TPU v7x, 32 devices: a whole 2x2x4 slice. The times are simulated.
32 devices in a mesh: blk: 2 (over x), dp: 16 (over z, y, core).
Axes of the slice: x: 2, y: 2, z: 4, core: 2. Of those that a mesh axis runs over, the one named last changes fastest.
Arguments:
- hidden: bfloat16 [16, 4096, 768], P('dp', 'blk'), may hold values from -6 to 6
- separators: int32 [16], P('dp'), may hold values from 1 to 4095, as said below
- out_grad: bfloat16 [16, 4096, 768], P('dp', 'blk'), may hold values from -6 to 6
- w_query: float32 [768, 384], P('dp'), may hold values from -0.21875 to 0.21875
- b_query: float32 [384], P('dp'), may hold values from -2 to 2
- w_key: float32 [768, 384], P('dp'), may hold values from -0.21875 to 0.21875
- w_value: float32 [768, 384], P('dp'), may hold values from -0.21875 to 0.21875
- b_value: float32 [384], P('dp'), may hold values from -2 to 2
- depth_kernel: float32 [768, 9], P('dp'), may hold values from -2 to 2
- w_point: float32 [768, 384], P('dp'), may hold values from -0.21875 to 0.21875
- b_keyconv: float32 [384], P('dp'), may hold values from -2 to 2
- w_kernel: float32 [384, 54], P('dp'), may hold values from -0.3125 to 0.3125
- kernel_bias: float32 [54], replicated, may hold values from -3 to 3
- w_convout: float32 [768, 384], P('dp'), may hold values from -0.21875 to 0.21875
- b_convout: float32 [384], P('dp'), may hold values from -2 to 2
- w_dense: float32 [768, 768], P('dp'), may hold values from -0.3125 to 0.3125
- b_dense: float32 [768], P('dp'), may hold values from -2 to 2
- gain_attn: float32 [768], P('dp'), may hold values from 0.5 to 1.5
- shift_attn: float32 [768], P('dp'), may hold values from -2 to 2
- w_up: float32 [2, 384, 1536], P(None, 'dp'), may hold values from -0.3125 to 0.3125
- b_up: float32 [3072], P('dp'), may hold values from -2 to 2
- w_down: float32 [2, 1536, 384], P(None, 'dp'), may hold values from -0.15625 to 0.15625
- b_down: float32 [768], P('dp'), may hold values from -2 to 2
- gain_out: float32 [768], P('dp'), may hold values from 0.5 to 1.5
- shift_out: float32 [768], P('dp'), may hold values from -2 to 2
Outputs:
- output: bfloat16 [16, 4096, 768], P('dp', 'blk')
- grad_hidden: bfloat16 [16, 4096, 768], P('dp', 'blk')
- grad_w_query: float32 [768, 384], P('dp')
- grad_b_query: float32 [384], P('dp')
- grad_w_key: float32 [768, 384], P('dp')
- grad_w_value: float32 [768, 384], P('dp')
- grad_b_value: float32 [384], P('dp')
- grad_depth_kernel: float32 [768, 9], P('dp')
- grad_w_point: float32 [768, 384], P('dp')
- grad_b_keyconv: float32 [384], P('dp')
- grad_w_kernel: float32 [384, 54], P('dp')
- grad_kernel_bias: float32 [54], replicated
- grad_w_convout: float32 [768, 384], P('dp')
- grad_b_convout: float32 [384], P('dp')
- grad_w_dense: float32 [768, 768], P('dp')
- grad_b_dense: float32 [768], P('dp')
- grad_gain_attn: float32 [768], P('dp')
- grad_shift_attn: float32 [768], P('dp')
- grad_w_up: float32 [2, 384, 1536], P(None, 'dp')
- grad_b_up: float32 [3072], P('dp')
- grad_w_down: float32 [2, 1536, 384], P(None, 'dp')
- grad_b_down: float32 [768], P('dp')
- grad_gain_out: float32 [768], P('dp')
- grad_shift_out: float32 [768], P('dp')
Inputs may be any that keep to these rules, and one draw needn't show every extreme that they name: Each row's second segment starts at its separator, so both segments are nonempty. Either all even rows or all odd rows, which ones drawn from the seed, have their separator below 2048 or above 2048; the other rows' separators may lie anywhere.
All inputs are finite; a program needn't handle non-finite values.
Results may differ from a plain program's by a relative error of at most 0.034.
Values may be sent and summed in bfloat16 or wider, within the bound.
A program may use at most 256 MiB of HBM per device.

v0:
```python
import functools, math
import jax, jax.numpy as jnp
from jax import lax
from jax.experimental import pallas as pl
from jax.experimental.pallas import tpu as pltpu
from jax.sharding import PartitionSpec as P

HEADS = 6
HD = 64
KSIZE = 9
REACH = 4
ATT = 384
EPS = 1e-12
BF = jnp.bfloat16
F32 = jnp.float32
MIB = 2**20
EXCLUDED = 2.0**100
SAFE_SCORE = 50.0


def mm(left, right):
    return jnp.dot(left, right, preferred_element_type=F32)


def mm_nt(left, right):
    return lax.dot_general(left, right, (((1,), (1,)), ((), ())), preferred_element_type=F32)


def mm_tn(left, right):
    return lax.dot_general(left, right, (((0,), (0,)), ((), ())), preferred_element_type=F32)


def in_lanes(rows, columns):
    lane = lax.broadcasted_iota(jnp.int32, (rows, 128), 1)
    out = jnp.zeros((rows, 128), F32)
    for at, column in enumerate(columns):
        out = jnp.where(lane == at, column, out)
    return out.astype(BF)


def in_rows(columns, rows):
    row = lax.broadcasted_iota(jnp.int32, (16, columns), 0)
    out = jnp.zeros((16, columns), F32)
    for at, values in enumerate(rows):
        out = jnp.where(row == at, values, out)
    return out.astype(BF)


def three_parts(values):
    high = values.astype(BF).astype(F32)
    rest = values - high
    middle = rest.astype(BF).astype(F32)
    return high, middle, (rest - middle).astype(BF).astype(F32)


def put_head(ref, head, values):
    odd = lax.rem(head, 2) == 1
    none = jnp.zeros_like(values)
    ref[0:HD, :] = jnp.where(odd, none, values)
    ref[HD : 2 * HD, :] = jnp.where(odd, values, none)


def attend_kernel(keys, queries, chunk, count, step, at_ref, q_ref, k_ref, v_ref, norm_ref, o_ref, p_ref, key_side, query_side):
    head, tile = pl.program_id(0), pl.program_id(1)
    separator, block = at_ref[0], lax.axis_index("blk")
    first_query = block * keys
    first_key = lax.rem(block + step, count) * keys

    @pl.when((head == 0) & (tile == 0))
    def start():
        position = first_key + lax.broadcasted_iota(jnp.int32, (keys, 128), 0)
        late = (position >= separator).astype(F32)
        key_side[...] = in_lanes(keys, [1.0 - late, late, 1.0, 1.0, 1.0])
        query_side[2 * HD + 16 :, :] = jnp.zeros((2 * HD - 16, queries), BF)

    put_head(query_side, head, q_ref[...])
    position = first_query + tile * queries + lax.broadcasted_iota(jnp.int32, (16, queries), 1)
    late = (position >= separator).astype(F32)
    excluded = [-EXCLUDED * late, -EXCLUDED * (1.0 - late)]
    query_side[2 * HD : 2 * HD + 16, :] = in_rows(queries, excluded)
    o_ref[0, HD + 8 : HD + 16, :] = jnp.zeros((8, queries), F32)
    wide = q_ref[...].astype(F32)
    largest = jnp.max(jnp.sum(wide * wide, axis=0, keepdims=True)) * jnp.max(norm_ref[...])

    def scores(at):
        part = slice(at * chunk, (at + 1) * chunk)
        return mm(
            jnp.concatenate([k_ref[part, :], key_side[part, :]], axis=1), query_side[...]
        )

    @pl.when(jnp.logical_not(largest <= SAFE_SCORE * SAFE_SCORE))
    def shifted():
        best = jnp.full((1, queries), -4.0 * EXCLUDED, F32)
        for at in range(keys // chunk):
            best = jnp.maximum(best, jnp.max(scores(at), axis=0, keepdims=True))
        parts = three_parts(jnp.where(best < -0.5 * EXCLUDED, 0.0, best))
        query_side[2 * HD : 2 * HD + 16, :] = in_rows(queries, excluded + [-part for part in parts])
        o_ref[0, HD + 8 : HD + 16, :] = jnp.broadcast_to(
            jnp.where(best < -0.5 * EXCLUDED, best, parts[0] + parts[1] + parts[2]), (8, queries)
        )

    ones = in_rows(chunk, [1.0])
    total = jnp.zeros((HD + 16, queries), F32)
    for at in range(keys // chunk):
        part = slice(at * chunk, (at + 1) * chunk)
        probs = jnp.exp(scores(at)).astype(BF)
        p_ref[0, part, :] = probs
        total = total + mm(jnp.concatenate([v_ref[:, part], ones], axis=0), probs)
    o_ref[0, 0 : HD + 8, :] = total[0 : HD + 8, :]


def attend(at, query_t, key, value_t, norms, count, step):
    tokens, keys = query_t.shape[1], key.shape[0]
    queries, chunk = math.gcd(tokens, 2048), math.gcd(keys, 1024)
    return pl.pallas_call(
        functools.partial(attend_kernel, keys, queries, chunk, count, step),
        grid=(HEADS, tokens // queries),
        in_specs=[
            pl.BlockSpec(memory_space=pltpu.SMEM),
            pl.BlockSpec((HD, queries), lambda h, i: (h, i)),
            pl.BlockSpec((keys, 2 * HD), lambda h, i: (0, h // 2)),
            pl.BlockSpec((HD, keys), lambda h, i: (h, 0)),
            pl.BlockSpec(norms.shape, lambda h, i: (0, 0)),
        ],
        out_specs=[
            pl.BlockSpec((1, HD + 16, queries), lambda h, i: (h, 0, i)),
            pl.BlockSpec((1, keys, queries), lambda h, i: (h, 0, i)),
        ],
        out_shape=[
            jax.ShapeDtypeStruct((HEADS, HD + 16, tokens), F32),
            jax.ShapeDtypeStruct((HEADS, keys, tokens), BF),
        ],
        scratch_shapes=[pltpu.VMEM((keys, 128), BF), pltpu.VMEM((4 * HD, queries), BF)],
        compiler_params=pltpu.CompilerParams(vmem_limit_bytes=56 * MIB),
        cost_estimate=pl.CostEstimate(
            flops=ATT * keys,
            bytes_accessed=2 * HEADS * keys,
            transcendentals=0,
        ),
        name="attend",
    )(at, query_t, key, value_t, norms)


def attend_back_kernel(first, keys, queries, chunk, p_ref, v_ref, kt_ref, g_ref, side_ref, q_ref, dq_ref, dkv_ref, value_side, grad_side, dk_sum, dv_sum):
    head, tile = pl.program_id(0), pl.program_id(1)

    @pl.when((head == 0) & (tile == 0))
    def start():
        value_side[...] = in_lanes(chunk, [1.0, 1.0, 1.0])
        grad_side[2 * HD + 16 :, :] = jnp.zeros((2 * HD - 16, queries), BF)

    @pl.when(tile == 0)
    def fresh():
        dk_sum[...] = jnp.zeros_like(dk_sum)
        dv_sum[...] = jnp.zeros_like(dv_sum)

    put_head(grad_side, first + head, g_ref[...])
    grad_side[2 * HD : 2 * HD + 16, :] = side_ref[0]
    total = jnp.zeros((HD, queries), F32)
    for at in range(keys // chunk):
        part = slice(at * chunk, (at + 1) * chunk)
        probs = p_ref[0, part, :]
        spread = mm(jnp.concatenate([v_ref[part, :], value_side[...]], axis=1), grad_side[...])
        grad_scores = (probs.astype(F32) * spread).astype(BF)
        dv_sum[:, part] += mm_nt(g_ref[...], probs)
        dk_sum[:, part] += mm_nt(q_ref[...], grad_scores)
        total = total + mm(kt_ref[:, part], grad_scores)
    dq_ref[...] = (total * (HD**-0.5)).astype(BF)

    @pl.when(tile == pl.num_programs(1) - 1)
    def finish():
        dkv_ref[0] = dk_sum[...].astype(BF)
        dkv_ref[1] = dv_sum[...].astype(BF)


def attend_back(probs, value, key_t, grad_t, side, query_t, first, heads):
    tokens, keys = query_t.shape[1], value.shape[0]
    queries, chunk = math.gcd(tokens, 1024), math.gcd(keys, 256)
    by_token = pl.BlockSpec((HD, queries), lambda h, i: (first + h, i))
    by_key = pl.BlockSpec((HD, keys), lambda h, i: (first + h, 0))
    return pl.pallas_call(
        functools.partial(attend_back_kernel, first, keys, queries, chunk),
        grid=(heads, tokens // queries),
        in_specs=[
            pl.BlockSpec((1, keys, queries), lambda h, i: (first + h, 0, i)),
            pl.BlockSpec((keys, 2 * HD), lambda h, i: (0, (first + h) // 2)),
            by_key,
            by_token,
            pl.BlockSpec((1, 16, queries), lambda h, i: (first + h, 0, i)),
            by_token,
        ],
        out_specs=[
            pl.BlockSpec((HD, queries), lambda h, i: (h, i)),
            pl.BlockSpec((2, HD, keys), lambda h, i: (0, h, 0)),
        ],
        out_shape=[
            jax.ShapeDtypeStruct((heads * HD, tokens), BF),
            jax.ShapeDtypeStruct((2, heads * HD, keys), BF),
        ],
        scratch_shapes=[
            pltpu.VMEM((chunk, 128), BF),
            pltpu.VMEM((4 * HD, queries), BF),
            pltpu.VMEM((HD, keys), F32),
            pltpu.VMEM((HD, keys), F32),
        ],
        compiler_params=pltpu.CompilerParams(vmem_limit_bytes=56 * MIB),
        cost_estimate=pl.CostEstimate(
            flops=32 * heads * HD * tokens * keys,
            bytes_accessed=2 * heads * tokens * keys,
            transcendentals=0,
        ),
        name="attend_back",
    )(probs, value, key_t, grad_t, side, query_t)


def all_of(shape):
    return pl.BlockSpec(shape, lambda *at: (0,) * len(shape))


def rows_of(rows, width):
    return pl.BlockSpec((rows, width), lambda i: (i, 0))


def columns_of(height, columns):
    return pl.BlockSpec((height, columns), lambda i: (0, i))


def run_tiles(kernel, name, steps, inputs, outputs, scratch, flops, aliases=None):
    args, in_specs = zip(*inputs)
    shapes, out_specs = zip(*outputs)
    size = sum(math.prod(v.shape) * v.dtype.itemsize for v in args + shapes)
    return pl.pallas_call(
        kernel,
        grid=(steps,),
        in_specs=list(in_specs),
        out_specs=list(out_specs),
        out_shape=list(shapes),
        scratch_shapes=scratch,
        input_output_aliases=aliases or {},
        compiler_params=pltpu.CompilerParams(vmem_limit_bytes=62 * MIB),
        cost_estimate=pl.CostEstimate(flops=flops, bytes_accessed=size, transcendentals=0),
        name=name,
    )(*args)


def shaped(shape, dtype):
    return jax.ShapeDtypeStruct(shape, dtype)


def project_kernel(parts, sources, *refs):
    x_refs, refs = refs[:sources], refs[sources:]
    (w_ref, thin_ref, thin_columns_ref), refs = refs[:3], refs[3:]
    norm_ref, flipped = refs[2 * parts], refs[2 * parts + 1]
    skip = (3 - parts) * ATT

    @pl.when(pl.program_id(0) == 0)
    def start():
        norm_ref[...] = jnp.zeros_like(norm_ref)
        flipped[...] = w_ref[:, skip:].T

    x = x_refs[-1][...]
    if sources == 2:
        x = jnp.where(pl.program_id(0) == 0, x_refs[0][...], x)
    plain = mm(x, w_ref[:, skip:])
    turned = mm_nt(flipped[...], x)
    for part in range(parts):
        own = slice(part * ATT, (part + 1) * ATT)
        bias, bias_t = 0.0, 0.0
        if part != parts - 2:
            at = 1 if part == parts - 1 else 0
            bias, bias_t = thin_ref[at : at + 1, :], thin_columns_ref[:, THIN_AT + at : THIN_AT + at + 1]
        refs[2 * part][...] = (plain[:, own] + bias).astype(BF)
        across = (turned[own] + bias_t).astype(BF)
        if part == parts - 2:
            wide = across.astype(F32)
            for head in range(HEADS):
                cells = wide[head * HD : (head + 1) * HD]
                size = jnp.sum(cells * cells, axis=0, keepdims=True)
                norm_ref[...] = jnp.maximum(norm_ref[...], size)
        if part < parts - 2:
            across = (across.astype(F32) * (HD**-0.5)).astype(BF)
        refs[2 * part + 1][...] = across


def project(sources, weight, thin, thin_columns, parts):
    tokens, width = sum(x.shape[0] for x in sources), sources[0].shape[1]
    wide = 3 * ATT
    tile = math.gcd(tokens, 512)
    late = len(sources) - 1
    inputs = [(sources[-1], pl.BlockSpec((tile, width), lambda i: (jnp.maximum(i - late, 0), 0)))]
    if late:
        inputs.insert(0, (sources[0], all_of((tile, width))))
    outputs = []
    for part in range(parts):
        outputs.append((shaped((tokens, ATT), BF), rows_of(tile, ATT)))
        outputs.append((shaped((ATT, tokens), BF), columns_of(ATT, tile)))
    outputs.append((shaped((8, tile), F32), all_of((8, tile))))
    return run_tiles(
        functools.partial(project_kernel, parts, len(sources)),
        "project",
        tokens // tile,
        inputs
        + [
            (weight, all_of((width, wide))),
            (thin, all_of(thin.shape)),
            (thin_columns, all_of(thin_columns.shape)),
        ],
        outputs,
        [pltpu.VMEM((parts * ATT, width), BF)],
        4 * tokens * width * parts * ATT,
    )


def fill_rows(window, x_ref, halo_ref, tile, tiles, rows):
    first = tile * rows
    tokens = x_ref.shape[0]
    before = x_ref[pl.ds(pl.multiple_of(jnp.maximum(first - 16, 0), 16), 16), :]
    after = x_ref[pl.ds(pl.multiple_of(jnp.minimum(first + rows, tokens - 16), 16), 16), :]
    window[0:16, :] = jnp.where(tile == 0, halo_ref[0:16, :], before).astype(window.dtype)
    window[16 : 16 + rows, :] = x_ref[pl.ds(pl.multiple_of(first, rows), rows), :].astype(window.dtype)
    window[16 + rows :, :] = jnp.where(
        tile == tiles - 1, halo_ref[16:32, :], after
    ).astype(window.dtype)


def fill_window(window, x_ref, halo_ref, tile, rows):
    fill_rows(window, x_ref, halo_ref, tile, pl.num_programs(0), rows)


def fill_spread(spread):
    row = lax.broadcasted_iota(jnp.int32, (128, ATT), 0)
    head = lax.broadcasted_iota(jnp.int32, (128, ATT), 1) // HD
    for tap in range(KSIZE):
        spread[:, tap * ATT : (tap + 1) * ATT] = (row == tap * 8 + head).astype(F32).astype(BF)


def mix_kernel(rows, count, x_ref, halo_ref, q_ref, wc_ref, wp_ref, wide_ref, thin_ref, wk_ref, bk_ref, depth_ref, keyconv_ref, attn_ref, kernt_ref, kern_ref, conv_ref, out_ref, rim_ref, window, conv_window, spread):
    tile = pl.program_id(0)
    last = pl.num_programs(0) - 1

    @pl.when(tile == 0)
    def start():
        fill_spread(spread)

    fill_window(window, x_ref, halo_ref, tile, rows)
    width = window.shape[1]
    for at in range(0, width, 128):
        some = slice(at, at + 128)
        total = jnp.zeros((rows, 128), F32)
        for tap in range(KSIZE):
            total = total + window[12 + tap : 12 + tap + rows, some] * wide_ref[TAPS_AT + tap : TAPS_AT + tap + 1, some]
        depth_ref[:, some] = total.astype(BF)
    position = (
        lax.axis_index("blk") * x_ref.shape[0] + tile * rows - 16 + lax.broadcasted_iota(jnp.int32, (rows + 32, ATT), 0)
    )
    inside = (position >= 0) & (position < count * x_ref.shape[0])
    values = mm(window[...].astype(BF), wc_ref[...]) + thin_ref[3:4, :]
    values = jnp.where(inside, values, 0.0).astype(BF)
    out_ref[...] = values[16 : 16 + rows]

    @pl.when(tile == 0)
    def first_rim():
        rim_ref[0:16, :] = values[0:16]

    @pl.when(tile == last)
    def last_rim():
        rim_ref[16:32, :] = values[16 + rows :]

    conv_window[...] = values.astype(F32)
    keyconv = mm(depth_ref[...], wp_ref[...]) + thin_ref[2:3, :]
    keyconv_ref[...] = keyconv
    attn_key = (keyconv * q_ref[...].astype(F32)).astype(BF)
    attn_ref[...] = attn_key
    logits = mm_nt(wk_ref[...], attn_key) + bk_ref[:, BIAS_AT : BIAS_AT + 1]
    slabs = [logits[8 * tap : 8 * tap + 8] for tap in range(KSIZE)]
    best = functools.reduce(jnp.maximum, slabs)
    slabs = [jnp.exp(slab - best) for slab in slabs]
    share = 1.0 / functools.reduce(jnp.add, slabs)
    slabs = [slab * share for slab in slabs]
    kernt = jnp.concatenate(slabs + [jnp.zeros((128 - 8 * KSIZE, rows), F32)], axis=0)
    kernt_ref[...] = kernt[0 : 8 * KSIZE]
    kern = kernt.astype(BF).T
    kern_ref[...] = kern
    total = jnp.zeros((rows, ATT), F32)
    for tap in range(KSIZE):
        total = total + mm(kern, spread[:, tap * ATT : (tap + 1) * ATT]) * conv_window[12 + tap : 12 + tap + rows, :]
    conv_ref[...] = total.astype(BF)


def column_block(weight, place):
    return pl.BlockSpec((weight.shape[0], ATT), lambda i: (0, place))


def mix(count, x, halo, query, weight, wide_vectors, thin, w_kernel, kernel_bias):
    tokens, width = x.shape
    rows = math.gcd(tokens, 512)
    whole = [(weight, column_block(weight, 2)), (weight, column_block(weight, 3))]
    whole += [(v, all_of(v.shape)) for v in (wide_vectors, thin, w_kernel, kernel_bias)]
    return run_tiles(
        functools.partial(mix_kernel, rows, count),
        "mix",
        tokens // rows,
        [
            (x, all_of(x.shape)),
            (halo, all_of(halo.shape)),
            (query, rows_of(rows, ATT)),
        ]
        + whole,
        [
            (shaped((tokens, width), BF), rows_of(rows, width)),
            (shaped((tokens, ATT), F32), rows_of(rows, ATT)),
            (shaped((tokens, ATT), BF), rows_of(rows, ATT)),
            (shaped((8 * KSIZE, tokens), F32), columns_of(8 * KSIZE, rows)),
            (shaped((tokens, 128), BF), rows_of(rows, 128)),
            (shaped((tokens, ATT), BF), rows_of(rows, ATT)),
            (shaped((tokens, ATT), BF), rows_of(rows, ATT)),
            (shaped((32, ATT), BF), all_of((32, ATT))),
        ],
        [
            pltpu.VMEM((rows + 32, width), F32),
            pltpu.VMEM((rows + 32, ATT), F32),
            pltpu.VMEM((128, KSIZE * ATT), BF),
        ],
        4 * tokens * width * ATT * 4,
    )


def normal(values):
    centre = values - jnp.mean(values, axis=-1, keepdims=True)
    scale = lax.rsqrt(jnp.mean(centre * centre, axis=-1, keepdims=True) + EPS)
    return centre * scale, scale


def normal_back(grad, unit, scale):
    return scale * (
        grad
        - jnp.mean(grad, axis=-1, keepdims=True)
        - unit * jnp.mean(grad * unit, axis=-1, keepdims=True)
    )


def gelu_parts(values):
    share = 0.5 + 0.5 * lax.erf(values * math.sqrt(0.5))
    bell = jnp.exp2(values * values * (-0.5 * math.log2(math.e)))
    return values * share, share + values * (bell * (1.0 / math.sqrt(2.0 * math.pi)))


def middle_kernel(blocks, rows, units, *refs):
    o_refs, refs = refs[:blocks], refs[blocks:]
    (conv_ref, x_ref, og_ref, wd_ref, late_ref, vec_ref, bu_ref), refs = refs[:7], refs[7:]
    (out_ref, sum_ref, gconv_ref), refs = refs[:3], refs[3:]
    g_refs, refs = refs[:blocks], refs[blocks:]
    side_refs, refs = refs[:blocks], refs[blocks:]
    (packed_ref, gvec_ref, gbu_ref, wd_sum, wu_sum, wn_sum, acts, slopes, staged, sems, wu_ref, wn_ref) = refs
    tile = pl.program_id(0)
    hidden_units = wu_ref.shape[1]
    groups = 2
    inner = ATT
    outer = hidden_units // groups

    @pl.when(tile == 0)
    def start():
        for ref in (wd_sum, wu_sum, wn_sum, gvec_ref, gbu_ref):
            ref[...] = jnp.zeros_like(ref)
        owners, high, width = late_ref.shape
        quarter = high // 8
        for pair in range(0, owners, 2):
            both = [late_ref[owner, 0 : high // 2].astype(F32) for owner in (pair, pair + 1)]
            for place in range(4):
                some = [cells[place * quarter : (place + 1) * quarter] for cells in both]
                wu_ref[pair * quarter : (pair + 2) * quarter, place * width : (place + 1) * width] = (
                    jnp.concatenate(some, axis=0).astype(BF)
                )
        for owner in range(owners):
            wn_ref[owner * high // 2 : (owner + 1) * high // 2] = late_ref[owner, high // 2 :]

    shifts = [ref[:, HD + 8 : HD + 9, :] for ref in o_refs]
    top = functools.reduce(jnp.maximum, shifts)
    weights = [jnp.exp(shift - top) for shift in shifts]
    mass = functools.reduce(jnp.add, [w * ref[:, HD : HD + 1, :] for w, ref in zip(weights, o_refs)])
    weights = [w / mass for w in weights]
    heads = functools.reduce(jnp.add, [w * ref[:, 0:HD, :] for w, ref in zip(weights, o_refs)])
    att_t = heads.reshape(ATT, rows).astype(BF)
    conv = conv_ref[...]
    vec = [vec_ref[at : at + 1, :] for at in range(6)]
    dense = mm(att_t.T, wd_ref[0:ATT, :]) + mm(conv, wd_ref[ATT:, :]) + vec[0]
    unit_one, scale_one = normal(dense + x_ref[...].astype(F32))
    normed = unit_one * vec[1] + vec[2]
    low = normed.astype(BF)
    downs = []
    for group in range(groups):
        mine = low[:, group * inner : (group + 1) * inner]
        down = jnp.zeros((rows, inner), F32)
        for at in range(0, outer, units):
            here = slice(group * outer + at, group * outer + at + units)
            upward = mm(mine, wu_ref[:, here]) + bu_ref[:, here]
            act, slope = gelu_parts(upward)
            act = act.astype(BF)
            acts[:, here] = act
            slopes[:, here] = slope.astype(BF)
            down = down + mm(act, wn_ref[at : at + units, group * inner : (group + 1) * inner])
        downs.append(down)
    unit_two, scale_two = normal(jnp.concatenate(downs, axis=1) + vec[3] + normed)
    out_ref[...] = (unit_two * vec[4] + vec[5]).astype(BF)
    og = og_ref[...].astype(F32)
    gvec_ref[4:5, :] += jnp.sum(og * unit_two, axis=0, keepdims=True)
    gvec_ref[5:6, :] += jnp.sum(og, axis=0, keepdims=True)
    grad_two = normal_back(og * vec[4], unit_two, scale_two)
    grad_down = grad_two.astype(BF)
    gvec_ref[3:4, :] += jnp.sum(grad_down.astype(F32), axis=0, keepdims=True)
    backs = []
    for group in range(groups):
        lanes = slice(group * inner, (group + 1) * inner)
        mine, grads = low[:, lanes], grad_down[:, lanes]
        mine_t = mine.T
        back = jnp.zeros((rows, inner), F32)
        for at in range(0, outer, units):
            here = slice(group * outer + at, group * outer + at + units)
            grad_act = mm_nt(grads, wn_ref[at : at + units, lanes])
            grad_up = (grad_act * slopes[:, here].astype(F32)).astype(BF)
            gbu_ref[0:1, here] += jnp.sum(grad_up.astype(F32), axis=0, keepdims=True)
            wn_sum[at : at + units, lanes] += mm_tn(acts[:, here], grads)
            wu_sum[:, here] += mm(mine_t, grad_up)
            back = back + mm_nt(grad_up, wu_ref[:, here])
        backs.append(back)
    grad_normed = grad_two + jnp.concatenate(backs, axis=1)
    gvec_ref[1:2, :] += jnp.sum(grad_normed * unit_one, axis=0, keepdims=True)
    gvec_ref[2:3, :] += jnp.sum(grad_normed, axis=0, keepdims=True)
    grad_one = normal_back(grad_normed * vec[1], unit_one, scale_one)
    sum_ref[...] = grad_one
    grad_dense = grad_one.astype(BF)
    gvec_ref[0:1, :] += jnp.sum(grad_dense.astype(F32), axis=0, keepdims=True)
    wd_sum[0:ATT, :] += mm(att_t, grad_dense)
    wd_sum[ATT:, :] += mm_tn(conv, grad_dense)
    gconv_ref[...] = mm_nt(grad_dense, wd_ref[ATT:, :]).astype(BF)
    grad_att = mm_nt(wd_ref[0:ATT, :], grad_dense).astype(BF).astype(F32).reshape(HEADS, HD, rows)
    for weight, g_ref, side_ref in zip(weights, g_refs, side_refs):
        share = (grad_att * weight).astype(BF)
        g_ref[...] = share.reshape(ATT, rows)
        delta = -jnp.sum(share.astype(F32) * heads, axis=1, keepdims=True)
        row = lax.broadcasted_iota(jnp.int32, (HEADS, 16, rows), 1)
        side = jnp.zeros((HEADS, 16, rows), F32)
        for at, part in enumerate(three_parts(delta)):
            side = jnp.where(row == at, part, side)
        side_ref[...] = side.astype(BF)

    @pl.when(tile == pl.num_programs(0) - 1)
    def finish():
        slots = staged.shape[0]
        sharers = packed_ref.shape[0]
        shard = wd_sum.shape[0] // sharers
        quarter = shard // 2
        width = wd_sum.shape[1]
        copies = []
        for owner in range(sharers):
            slot = owner % slots
            if owner >= slots:
                copies[owner - slots].wait()
            staged[slot, 0:shard] = wd_sum[owner * shard : (owner + 1) * shard].astype(BF)
            some = wu_sum[owner * quarter : (owner + 1) * quarter]
            for group in range(groups):
                pair = [some[:, at : at + width] for at in (2 * group * width, (2 * group + 1) * width)]
                staged[slot, (1 + group) * shard : (2 + group) * shard] = jnp.concatenate(pair, axis=0).astype(BF)
            some = wn_sum[owner * 2 * shard : (owner + 1) * 2 * shard]
            staged[slot, 3 * shard : 5 * shard] = some.astype(BF)
            copy = pltpu.make_async_copy(
                staged.at[slot], packed_ref.at[owner, 0 : 5 * shard], sems.at[owner]
            )
            copy.start()
            copies.append(copy)
        for copy in copies[sharers - slots :]:
            copy.wait()


def middle(outs, conv, x, out_grad, w_dense, late, vectors, b_up):
    tokens, width = x.shape
    sharers = late.shape[0]
    shard = width // sharers
    units = b_up.shape[1]
    up, down = (width // 2, units), (units // 2, width)
    rows = math.gcd(tokens, 512)
    blocks = len(outs)
    heads = pl.BlockSpec((HEADS, HD + 16, rows), lambda i: (0, 0, i))
    side = pl.BlockSpec((HEADS, 16, rows), lambda i: (0, 0, i))
    single = pl.Buffered(1)
    once = [
        (w_dense, pl.BlockSpec((width, width), lambda i: (0, 0), pipeline_mode=single)),
        (late, pl.BlockSpec(late.shape, lambda i: (0, 0, 0), pipeline_mode=single)),
    ]
    once += [(v, all_of(v.shape)) for v in (vectors, b_up)]
    results = run_tiles(
        functools.partial(middle_kernel, blocks, rows, 768),
        "middle",
        tokens // rows,
        [(o, heads) for o in outs]
        + [
            (conv, rows_of(rows, ATT)),
            (x, rows_of(rows, width)),
            (out_grad, rows_of(rows, width)),
        ]
        + once,
        [
            (shaped((tokens, width), BF), rows_of(rows, width)),
            (shaped((tokens, width), F32), rows_of(rows, width)),
            (shaped((tokens, ATT), BF), rows_of(rows, ATT)),
        ]
        + [(shaped((ATT, tokens), BF), columns_of(ATT, rows))] * blocks
        + [(shaped((HEADS, 16, tokens), BF), side)] * blocks
        + [
            (shaped((sharers, 7 * shard, width), BF), pl.BlockSpec(memory_space=pl.ANY)),
            (shaped((8, width), F32), all_of((8, width))),
            (shaped((8, units), F32), all_of((8, units))),
        ],
        [
            pltpu.VMEM((width, width), F32),
            pltpu.VMEM(up, F32),
            pltpu.VMEM(down, F32),
            pltpu.VMEM((rows, units), BF),
            pltpu.VMEM((rows, units), BF),
            pltpu.VMEM((2, 5 * shard, width), BF),
            pltpu.SemaphoreType.DMA((sharers,)),
            pltpu.VMEM(up, BF),
            pltpu.VMEM(down, BF),
        ],
        6 * tokens * (width * width + 2 * math.prod(up)),
    )
    output, grad_sum, grad_conv = results[:3]
    return output, grad_sum, grad_conv, results[3 : 3 + blocks], results[3 + blocks : 3 + 2 * blocks], results[3 + 2 * blocks :]


def mix_back_kernel(rows, count, x_ref, halo_ref, values_ref, rim_ref, gconv_ref, kernt_ref, kern_ref, q_ref, keyconv_ref, attn_ref, depth_ref, wp_ref, wk_ref, gvec_ref, gbu_ref, unused, gq_ref, gdepth_ref, gvalues_ref, packed_ref, turned_ref, window, conv_window, summed, products, spread, wp_sum, wc_sum, values_sum, gwk_ref, gbias_ref, gtaps_ref, turn_wide, turn_thin, side, staged, sem):
    tile = pl.program_id(0)

    @pl.when(tile == 0)
    def start():
        fill_spread(spread)
        for ref in (values_sum, wp_sum, wc_sum, gwk_ref, gbias_ref, gtaps_ref, turn_wide, turn_thin):
            ref[...] = jnp.zeros_like(ref)

    fill_window(window, x_ref, halo_ref, tile, rows)
    fill_window(conv_window, values_ref, rim_ref, tile, rows)
    summed[...] = jnp.zeros_like(summed)
    grad_conv = gconv_ref[...].astype(F32)
    for tap in range(KSIZE):
        here = slice(tap * ATT, (tap + 1) * ATT)
        there = slice(12 + tap, 12 + tap + rows)
        products[:, here] = (grad_conv * conv_window[there, :]).astype(BF)
        summed[there, :] += mm(kern_ref[...], spread[:, here]) * grad_conv
    first = pl.multiple_of(tile * rows, rows)
    values_sum[pl.ds(first, rows + 32), :] += summed[...]
    turned = x_ref[pl.ds(first, rows), :].T
    turned_ref[...] = turned
    edges = [slice(0, 16), slice(rows + 16, rows + 32)]
    edge_x = jnp.concatenate([window[edge, :] for edge in edges], axis=0).astype(BF)
    edge_grads = jnp.concatenate([summed[edge, :] for edge in edges], axis=0).astype(BF)
    wc_sum[...] += mm(turned, summed[16 : 16 + rows, :].astype(BF)) + mm_tn(edge_x, edge_grads)
    grad_kernel = mm_nt(spread[...], products[...])
    slabs = [slice(8 * tap, 8 * tap + 8) for tap in range(KSIZE)]
    kernels = [kernt_ref[slab, :] for slab in slabs]
    mean = functools.reduce(jnp.add, [k * grad_kernel[slab] for k, slab in zip(kernels, slabs)])
    grad_logits = jnp.concatenate(
        [k * (grad_kernel[slab] - mean) for k, slab in zip(kernels, slabs)], axis=0
    ).astype(BF)
    wide_logits = grad_logits.astype(F32)
    gbias_ref[...] += jnp.concatenate(
        [
            jnp.broadcast_to(jnp.sum(wide_logits, axis=1, keepdims=True), (8 * KSIZE, 128)),
            jnp.zeros((8, 128), F32),
        ],
        axis=0,
    )
    gwk_ref[0 : 8 * KSIZE, :] += mm(grad_logits, attn_ref[...])
    grad_attn = mm_tn(grad_logits, wk_ref[...]).astype(BF).astype(F32)
    grad_keyconv = (grad_attn * q_ref[...].astype(F32)).astype(BF)
    gq_ref[...] = (grad_attn * keyconv_ref[...]).astype(BF)
    gwk_ref[8 * KSIZE : 8 * KSIZE + 1, :] += jnp.sum(grad_keyconv.astype(F32), axis=0, keepdims=True)
    wp_sum[...] += mm_tn(depth_ref[...], grad_keyconv)
    grad_depth = mm_nt(grad_keyconv, wp_ref[...]).astype(BF)
    gdepth_ref[...] = grad_depth
    wide = grad_depth.astype(F32)
    for at in range(0, window.shape[1], 128):
        some = slice(at, at + 128)
        for tap in range(KSIZE):
            gtaps_ref[tap : tap + 1, some] += jnp.sum(
                wide[:, some] * window[12 + tap : 12 + tap + rows, some], axis=0, keepdims=True
            )

    @pl.when(tile == pl.num_programs(0) - 1)
    def finish():
        gvalues_ref[...] = values_sum[...].astype(BF)
        tokens, block = x_ref.shape[0], lax.axis_index("blk")
        sums = [
            jnp.sum(gvalues_ref[at:end, :].astype(F32), axis=0, keepdims=True)
            for at, end in ((0, 16), (16, tokens + 16), (tokens + 16, tokens + 32))
        ]
        b_sum = sums[1] + jnp.where(block > 0, sums[0], 0.0) + jnp.where(block < count - 1, sums[2], 0.0)
        sharers, shard, width = staged.shape[0], staged.shape[1] // 2, staged.shape[2]
        part = ATT // sharers
        half = gbu_ref.shape[1] // sharers // 2
        turn_wide[0:6, :] = gvec_ref[0:6, :]
        turn_wide[TAPS_AT : TAPS_AT + KSIZE, :] = gtaps_ref[0:KSIZE, :]
        vectors = turn_wide[...].T
        for h in range(HEADS):
            for j in range(KSIZE):
                turn_wide[h * KSIZE + j : h * KSIZE + j + 1, 0:LANES] = gbias_ref[j * 8 + h : j * 8 + h + 1, :]
                turn_thin[h * KSIZE + j : h * KSIZE + j + 1, :] = gwk_ref[j * 8 + h : j * 8 + h + 1, :]
        bias = turn_wide[:, 0:LANES].T[0:1]
        turn_thin[THIN_AT : THIN_AT + 1, :] = gwk_ref[8 * KSIZE : 8 * KSIZE + 1, :]
        turn_thin[THIN_AT + 1 : THIN_AT + 2, :] = b_sum
        kernels = turn_thin[...].T
        side[...] = jnp.zeros_like(side)
        for owner in range(sharers):
            staged[owner, 0:shard, 0:ATT] = wp_sum[owner * shard : (owner + 1) * shard].astype(BF)
            staged[owner, shard:, 0:ATT] = wc_sum[owner * shard : (owner + 1) * shard].astype(BF)
            staged[owner, shard:, ATT:] = jnp.zeros((shard, width - ATT), BF)
            staged[owner, 0:shard, ATT : ATT + LANES] = vectors[owner * shard : (owner + 1) * shard].astype(BF)
            side[0:part, :] = kernels[owner * part : (owner + 1) * part]
            for place in range(2):
                first = (2 * owner + place) * half
                side[part + place : part + place + 1, 0:half] = gbu_ref[0:1, first : first + half]
            side[part + 2 : part + 3, :] = bias
            staged[owner, 0:shard, ATT + LANES : ATT + 2 * LANES] = side[...].astype(BF)
            staged[owner, 0:shard, ATT + 2 * LANES :] = jnp.zeros((shard, width - ATT - 2 * LANES), BF)
        copy = pltpu.make_async_copy(staged, packed_ref.at[:, 5 * shard : 7 * shard], sem)
        copy.start()
        copy.wait()


def mix_back(count, x, halo, values, rim, grad_conv, kernt, kern, query, keyconv, attn_key, depth, weight, w_kernel, g_vectors, gb_up, packed):
    tokens, width = x.shape
    sharers, shard = packed.shape[0], packed.shape[1] // 7
    away = pl.BlockSpec(memory_space=pl.ANY)
    rows = math.gcd(tokens, 512)
    by_rows = [(v, rows_of(rows, v.shape[1])) for v in (kern, query, keyconv, attn_key, depth)]
    return run_tiles(
        functools.partial(mix_back_kernel, rows, count),
        "mix_back",
        tokens // rows,
        [(v, all_of(v.shape)) for v in (x, halo, values, rim)]
        + [(grad_conv, rows_of(rows, ATT)), (kernt, columns_of(8 * KSIZE, rows))]
        + by_rows
        + [(weight, column_block(weight, 3))]
        + [(v, all_of(v.shape)) for v in (w_kernel, g_vectors, gb_up)]
        + [(packed, away)],
        [
            (shaped((tokens, ATT), BF), rows_of(rows, ATT)),
            (shaped((tokens, width), BF), rows_of(rows, width)),
            (shaped((tokens + 32, ATT), BF), all_of((tokens + 32, ATT))),
            (shaped(packed.shape, BF), away),
            (shaped((width, tokens), BF), columns_of(width, rows)),
        ],
        [
            pltpu.VMEM((rows + 32, width), F32),
            pltpu.VMEM((rows + 32, ATT), F32),
            pltpu.VMEM((rows + 32, ATT), F32),
            pltpu.VMEM((rows, KSIZE * ATT), BF),
            pltpu.VMEM((128, KSIZE * ATT), BF),
            pltpu.VMEM((width, ATT), F32),
            pltpu.VMEM((width, ATT), F32),
            pltpu.VMEM((tokens + 32, ATT), F32),
            pltpu.VMEM((8 * KSIZE + 8, ATT), F32),
            pltpu.VMEM((8 * KSIZE + 8, LANES), F32),
            pltpu.VMEM((16, width), F32),
            pltpu.VMEM((LANES, width), F32),
            pltpu.VMEM((LANES, ATT), F32),
            pltpu.VMEM((shard, LANES), F32),
            pltpu.VMEM((sharers, 2 * shard, width), BF),
            pltpu.SemaphoreType.DMA(()),
        ],
        4 * tokens * width * ATT * 4,
        {15: 3},
    )


MESH = pl.DeviceIdType.MESH
LINE = 4
LANES = 128
TAPS_AT = 16
THIN_AT = 64
BIAS_AT = 100


def my_place(sharers):
    columns = sharers // (2 * LINE)
    me = lax.axis_index("dp")
    return me, me // (2 * columns), lax.rem(me // 2, columns), lax.rem(me, 2), columns


def greet(partners):
    barrier = pltpu.get_barrier_semaphore()
    for partner in partners:
        pl.semaphore_signal(barrier, inc=1, device_id=partner, device_id_type=MESH)
    return barrier


def remote(source, target, send_sem, recv_sem, device):
    return pltpu.make_async_remote_copy(
        src_ref=source,
        dst_ref=target,
        send_sem=send_sem,
        recv_sem=recv_sem,
        device_id=device,
        device_id_type=MESH,
    )


def gather_kernel(sharers, count, part, early, *refs):
    w_refs, refs = refs[:3], refs[3:]
    vector_refs, refs = refs[:6], refs[6:]
    thin_refs, refs = refs[:4], refs[4:]
    (taps_ref, up_ref, kernel_ref, bias_ref, wu_ref, wn_ref, head_ref, tail_ref, early_ref), refs = refs[:9], refs[9:]
    (out_ref, wide_ref, thin_ref, thin_columns_ref, bias_up_ref, wk_ref, bk_ref, halo_ref, late_out, early_out), refs = refs[:10], refs[10:]
    rows, side, flat, thin_flat, edges, send_sem, recv_sem, edge_send, edge_recv = refs
    me, line, column, core, columns = my_place(sharers)
    block = lax.axis_index("blk")
    shard = out_ref.shape[1]
    base = len(w_refs) * ATT
    half = up_ref.shape[0] // 2

    def at(line, column, core):
        return (line * columns + column) * 2 + core

    lines = [lax.rem(line + step, LINE) for step in range(1, LINE)]
    sides = [lax.rem(column + step, columns) for step in range(1, columns)]
    partners = [{"dp": at(other, column, core)} for other in lines]
    across = [{"dp": at(line, other, core)} for other in sides]
    mate = {"dp": at(line, column, 1 - core)}
    ends = []
    if count > 1:
        ends = [{"blk": lax.rem(block + 1, count)}, {"blk": lax.rem(block + count - 1, count)}]
    barrier = greet(partners + across + [mate] + ends)
    for place, ref in enumerate(w_refs):
        out_ref[me, :, place * ATT : (place + 1) * ATT] = ref[...].astype(BF)
    rows[...] = jnp.zeros_like(rows)
    for place, ref in enumerate(vector_refs):
        rows[place : place + 1, 0:shard] = ref[...].reshape(1, shard)
    for place, ref in enumerate(thin_refs):
        rows[THIN_AT + place : THIN_AT + place + 1, 0:part] = ref[...].reshape(1, part)
    rows[TAPS_AT : TAPS_AT + KSIZE, 0:shard] = taps_ref[...]
    rows[BIAS_AT : BIAS_AT + 1, 0 : HEADS * KSIZE] = bias_ref[...].reshape(1, HEADS * KSIZE)
    rows[...] = rows[...].T
    side[...] = rows[0:shard]
    out_ref[me, :, base : base + LANES] = side[...].astype(BF)
    side[...] = jnp.zeros_like(side)
    side[0:part, 0 : HEADS * KSIZE] = kernel_ref[...]
    side[part : part + 1, 0:half] = up_ref[0:half].reshape(1, half)
    side[part + 1 : part + 2, 0:half] = up_ref[half:].reshape(1, half)
    out_ref[me, :, base + LANES :] = side[...].astype(BF)
    width = late_out.shape[1]
    for group in range(2):
        pair = [wu_ref[group, :, place * width : (place + 1) * width] for place in range(2)]
        late_out[group * shard : (group + 1) * shard] = jnp.concatenate(pair, axis=0).astype(BF)
        late_out[2 * shard :, group * ATT : (group + 1) * ATT] = wn_ref[group].astype(BF)
    if not early:
        early_out[...] = early_ref[...]
    pl.semaphore_wait(barrier, len(partners) + len(across) + 1 + len(ends))
    sends = []

    def sending(number, owner, device):
        return remote(out_ref.at[owner], out_ref.at[owner], send_sem.at[number], recv_sem.at[owner], device)

    def pass_on(owner, devices, when=None):
        for device in devices:
            sending(len(sends), owner, device).start()
            sends.append((owner, device, when))

    def arrived(owner):
        pltpu.make_async_copy(out_ref.at[owner], out_ref.at[owner], recv_sem.at[owner]).wait()

    pass_on(me, across + [mate])
    edge_copies = []
    for place, (ref, device) in enumerate(zip((tail_ref, head_ref), ends)):
        edge_copies.append(remote(ref, edges.at[place], edge_send.at[place], edge_recv.at[place], device))
    if early:
        edge_copies.append(remote(early_ref, early_out, edge_send.at[2], edge_recv.at[2], ends[0]))
    for copy in edge_copies:
        copy.start()
    for step in range(1, LINE):
        for way in (1, -1):
            from_here = (line - way * (step - 1) >= 0) & (line - way * (step - 1) < LINE)
            goes = from_here & (line + way >= 0) & (line + way < LINE)
            owner, onward = at(line - way * (step - 1), column, core), [{"dp": at(line + way, column, core)}]

            @pl.when(goes)
            def forward():
                pass_on(owner, onward, goes)

        for way in (1, -1):
            comes = (line - way * step >= 0) & (line - way * step < LINE)
            owner = at(line - way * step, column, core)

            @pl.when(comes)
            def take():
                arrived(owner)
                pass_on(owner, across + [mate], comes)

    for some in sides:
        for other in [line] + lines:
            owner = at(other, some, core)
            arrived(owner)
            pass_on(owner, [mate])
    nothing = jnp.zeros((16, halo_ref.shape[1]), BF)
    halo_ref[0:16, :] = nothing
    halo_ref[16:32, :] = nothing
    if count > 1:
        for copy in edge_copies:
            copy.wait()
        halo_ref[0:16, :] = jnp.where(block > 0, edges[0], nothing)
        halo_ref[16:32, :] = jnp.where(block < count - 1, edges[1], nothing)
    for j in range(KSIZE):
        for h in range(8):
            source = h * KSIZE + j if h < HEADS else 120
            bk_ref[j * 8 + h : j * 8 + h + 1, :] = rows[source : source + 1, :]
    for some in [column] + sides:
        for other in [line] + lines:
            arrived(at(other, some, 1 - core))
    for number, (owner, device, when) in enumerate(sends):
        if when is None:
            sending(number, owner, device).wait_send()
        else:
            pl.when(when)(lambda: sending(number, owner, device).wait_send())
    for owner in range(sharers):
        cells = out_ref[owner, :, base : base + LANES].astype(F32)
        flat[owner * shard : (owner + 1) * shard, :] = cells
        thin_flat[owner * part : (owner + 1) * part, :] = cells[0:part]
    turned = flat[...].T
    wide_ref[...] = turned[0 : wide_ref.shape[0]]
    thin_columns_ref[...] = thin_flat[...]
    thin_ref[...] = thin_flat[...].T[THIN_AT : THIN_AT + 8]
    for owner in range(sharers):
        cells = out_ref[owner, :, base + LANES :].astype(F32)
        thin_flat[owner * part : (owner + 1) * part, :] = cells[0:part]
        for place in range(2):
            first = (2 * owner + place) * half
            bias_up_ref[0:1, first : first + half] = cells[part + place : part + place + 1, 0:half]
    turned = thin_flat[...].T
    slabs = []
    for j in range(KSIZE):
        slabs += [turned[h * KSIZE + j : h * KSIZE + j + 1] for h in range(HEADS)]
        slabs.append(jnp.zeros((8 - HEADS, ATT), F32))
    wk_ref[...] = jnp.concatenate(slabs, axis=0).astype(BF)


def gather_columns(weights, vectors, thin, taps, b_up, w_kernel, kernel_bias, w_up, w_down, x, sharers, count):
    shard, part = weights[0].shape[0], thin[0].shape[0]
    tokens, width = x.shape
    early = count == 2
    first_rows = math.gcd(tokens, 512) if early else 16
    wide = len(weights) * ATT + 2 * LANES
    columns = sharers // (2 * LINE)
    copies = columns + 2 * (LINE - 1) * (1 + columns) + LINE * (columns - 1)
    args = list(weights) + list(vectors) + list(thin) + [taps, b_up, w_kernel, kernel_bias, w_up, w_down]
    shapes = [
        shaped((sharers, shard, wide), BF),
        shaped((32, width), F32),
        shaped((8, ATT), F32),
        shaped((ATT, LANES), F32),
        shaped((1, sharers * b_up.shape[0]), F32),
        shaped((8 * KSIZE, ATT), BF),
        shaped((8 * KSIZE, LANES), F32),
        shaped((32, width), BF),
        shaped((4 * shard, width), BF),
        shaped((first_rows, width), BF),
    ]
    out, *rest = pl.pallas_call(
        functools.partial(gather_kernel, sharers, count, part, early),
        grid=(1,),
        in_specs=[all_of(v.shape) for v in args]
        + [
            pl.BlockSpec((16, width), lambda i: (0, 0)),
            pl.BlockSpec((16, width), lambda i: (tokens // 16 - 1, 0)),
            pl.BlockSpec((first_rows, width), lambda i: (0, 0)),
        ],
        out_specs=[all_of(v.shape) for v in shapes],
        out_shape=shapes,
        scratch_shapes=[
            pltpu.VMEM((LANES, LANES), F32),
            pltpu.VMEM((shard, LANES), F32),
            pltpu.VMEM((width, LANES), F32),
            pltpu.VMEM((ATT, LANES), F32),
            pltpu.VMEM((2, 16, width), BF),
            pltpu.SemaphoreType.DMA((copies,)),
            pltpu.SemaphoreType.DMA((sharers,)),
            pltpu.SemaphoreType.DMA((3,)),
            pltpu.SemaphoreType.DMA((3,)),
        ],
        compiler_params=pltpu.CompilerParams(
            collective_id=0, has_side_effects=True, vmem_limit_bytes=60 * MIB
        ),
        name="gather_columns",
    )(*args, x, x, x)
    return (out.reshape(sharers * shard, wide), *rest)


class Shares:
    def __init__(self, sharers, rows, widths, line_first, count):
        self.sharers, self.rows, self.widths, self.line_first, self.count = sharers, rows, widths, line_first, count
        self.columns = sharers // (2 * LINE)
        self.chips = sharers // 2
        ends = [sum(widths[: at + 1]) for at in range(len(widths))]
        self.lanes = [slice(end - width, end) for end, width in zip(ends, widths)]
        self.wide = ends[-1]
        self.copies = 1 + self.columns - 1 + LINE - 1 + count - 1

    def scratch(self):
        shapes = []
        for width, line_first in zip(self.widths, self.line_first):
            side = (self.columns - 1, 1 if line_first else LINE, self.rows, width)
            line = (LINE - 1, self.columns if line_first else 1, self.rows, width)
            shapes += [pltpu.VMEM((self.chips, self.rows, width), BF)] * 2
            shapes += [pltpu.VMEM(side, BF)] * 2 + [pltpu.VMEM(line, BF)] * 2
            shapes += [pltpu.VMEM((self.rows, width), BF), pltpu.VMEM((self.count, self.rows, width), BF)]
        sems = len(self.widths) * self.copies
        return shapes + [
            pltpu.VMEM((self.sharers, self.rows, self.wide), F32),
            pltpu.SemaphoreType.DMA((sems,)),
            pltpu.SemaphoreType.DMA((sems,)),
        ]

    def bind(self, refs):
        chains = len(self.widths)
        self.buffers = [refs[8 * chain : 8 * chain + 8] for chain in range(chains)]
        self.total, self.send_sem, self.recv_sem = refs[8 * chains : 8 * chains + 3]
        self.me, self.line, self.column, self.core, unused = my_place(self.sharers)
        self.block = lax.axis_index("blk")
        self.others_line = [lax.rem(self.line + step, LINE) for step in range(1, LINE)]
        self.others_side = [lax.rem(self.column + step, self.columns) for step in range(1, self.columns)]
        self.others_block = [lax.rem(self.block + step, self.count) for step in range(1, self.count)]

    def at(self, line, column, core):
        return (line * self.columns + column) * 2 + core

    def greet(self):
        devices = [{"dp": self.at(self.line, self.column, 1 - self.core)}]
        devices += [{"dp": self.at(self.line, other, self.core)} for other in self.others_side]
        devices += [{"dp": self.at(other, self.column, self.core)} for other in self.others_line]
        devices += [{"blk": other} for other in self.others_block]
        greet(devices)

    def met(self):
        pl.semaphore_wait(pltpu.get_barrier_semaphore(), 1 + self.columns - 1 + LINE - 1 + self.count - 1)

    def copy(self, chain, number, source, target, device):
        sem = chain * self.copies + number
        return remote(source, target, self.send_sem.at[sem], self.recv_sem.at[sem], device)

    def part(self, owner, chain):
        return self.total[owner, :, self.lanes[chain]]

    def add(self, owner, chain, values):
        self.total[owner, :, self.lanes[chain]] += values.astype(F32)

    def mate_copy(self, chain):
        mate = {"dp": self.at(self.line, self.column, 1 - self.core)}
        return self.copy(chain, 0, self.buffers[chain][0], self.buffers[chain][1], mate)

    def mate_start(self, chain):
        for chip in range(self.chips):
            self.buffers[chain][0][chip] = self.part(2 * chip + 1 - self.core, chain).astype(BF)
        self.mate_copy(chain).start()

    def mate_end(self, chain):
        self.mate_copy(chain).wait()
        for chip in range(self.chips):
            self.add(2 * chip + self.core, chain, self.buffers[chain][1][chip])

    def side_copies(self, chain):
        source, target = self.buffers[chain][2:4]
        return [
            self.copy(chain, 1 + step, source.at[step], target.at[step], {"dp": self.at(self.line, other, self.core)})
            for step, other in enumerate(self.others_side)
        ]

    def side_lines(self, chain):
        return [self.line] if self.line_first[chain] else range(LINE)

    def side_start(self, chain):
        for step, other in enumerate(self.others_side):
            for place, line in enumerate(self.side_lines(chain)):
                self.buffers[chain][2][step, place] = self.part(self.at(line, other, self.core), chain).astype(BF)
        for copy in self.side_copies(chain):
            copy.start()

    def side_end(self, chain):
        for step, copy in enumerate(self.side_copies(chain)):
            copy.wait()
            for place, line in enumerate(self.side_lines(chain)):
                self.add(self.at(line, self.column, self.core), chain, self.buffers[chain][3][step, place])

    def line_copies(self, chain):
        source, target = self.buffers[chain][4:6]
        return [
            self.copy(chain, self.columns + step, source.at[step], target.at[step], {"dp": self.at(other, self.column, self.core)})
            for step, other in enumerate(self.others_line)
        ]

    def line_columns(self, chain):
        return range(self.columns) if self.line_first[chain] else [self.column]

    def line_start(self, chain):
        for step, other in enumerate(self.others_line):
            for place, column in enumerate(self.line_columns(chain)):
                self.buffers[chain][4][step, place] = self.part(self.at(other, column, self.core), chain).astype(BF)
        for copy in self.line_copies(chain):
            copy.start()

    def line_end(self, chain):
        for step, copy in enumerate(self.line_copies(chain)):
            copy.wait()
            for place, column in enumerate(self.line_columns(chain)):
                self.add(self.at(self.line, column, self.core), chain, self.buffers[chain][5][step, place])

    def block_copies(self, chain):
        source, target = self.buffers[chain][6:8]
        return [
            self.copy(chain, self.columns + LINE - 1 + step, source, target.at[self.block], {"blk": other})
            for step, other in enumerate(self.others_block)
        ]

    def block_start(self, chain):
        own = self.part(self.me, chain).astype(BF)
        self.buffers[chain][6][...] = own
        self.buffers[chain][7][self.block] = own
        for copy in self.block_copies(chain):
            copy.start()

    def block_end(self, chain):
        for copy in self.block_copies(chain):
            copy.wait()
        parts = [self.buffers[chain][7][at].astype(F32) for at in range(self.count)]
        return functools.reduce(jnp.add, parts)


def finish_kernel(blocks, rows, tiles, shares, *refs):
    dq_refs, refs = refs[:blocks], refs[blocks:]
    dkv_refs, refs = refs[:blocks], refs[blocks:]
    (x_ref, gq_ref, gvalues_ref, gdepth_ref, w_ref, wc_ref, mine_ref, wide_ref, sum_ref), refs = refs[:9], refs[9:]
    (gh_ref, flat_out, sums_out), refs = refs[:3], refs[3:]
    held, refs = refs[: 2 * blocks + 5], refs[2 * blocks + 5 :]
    dq, dkv = held[:blocks], held[blocks : 2 * blocks]
    dk, dv = [ref.at[0] for ref in dkv], [ref.at[1] for ref in dkv]
    turned, gq, gvalues, gdepth, w = held[2 * blocks :]
    (load_sem, grads, window, bias_sum, rim_in, halo_in, halo, given, edge_send, edge_recv, given_send, given_recv), refs = refs[:12], refs[12:]
    shares.bind(refs)
    step = pl.program_id(0)
    count, sharers, shard = shares.count, shares.sharers, shares.rows
    chains = 3
    width, tokens = turned.shape
    block = shares.block
    sources = [x_ref, gq_ref] + list(dq_refs) + [ref.at[1] for ref in dkv_refs] + [ref.at[0] for ref in dkv_refs]
    targets = [turned, gq] + list(dq) + list(dv) + list(dk)
    sources += [gvalues_ref, gdepth_ref, w_ref.at[:, 0 : 3 * ATT], wc_ref.at[:, 2 * ATT : 3 * ATT]]
    targets += [gvalues, gdepth, w.at[:, 0 : 3 * ATT], w.at[:, 3 * ATT :]]
    loads = [
        pltpu.make_async_copy(source, target, load_sem.at[at])
        for at, (source, target) in enumerate(zip(sources, targets))
    ]
    by_chain = [loads[: 2 + blocks], loads[2 + blocks : 2 + 2 * blocks], loads[2 + 2 * blocks : 2 + 3 * blocks]]
    others = loads[2 + 3 * blocks :]

    def edge_copies():
        if count == 1:
            return []
        after, before = {"blk": lax.rem(block + 1, count)}, {"blk": lax.rem(block + count - 1, count)}
        plan = [
            (gvalues.at[tokens + 16 : tokens + 32], rim_in.at[0], after),
            (gvalues.at[0:16], rim_in.at[1], before),
            (gdepth.at[tokens - 16 : tokens], halo_in.at[0], after),
            (gdepth.at[0:16], halo_in.at[1], before),
        ]
        return [
            remote(source, target, edge_send.at[at], edge_recv.at[at], device)
            for at, (source, target, device) in enumerate(plan)
        ]

    def given_copies():
        return [
            remote(mine_ref, given.at[block], given_send.at[at], given_recv.at[at], {"blk": other})
            for at, other in enumerate(shares.others_block)
        ]

    @pl.when(step == 0)
    def start():
        shares.greet()
        for load in loads:
            load.start()
        bias_sum[...] = jnp.zeros_like(bias_sum)
        given[block] = mine_ref[...]

    def total(some):
        whole = [ref[...].astype(F32) for ref in some if ref.shape[0] == ATT]
        halves = [ref[...].astype(F32) for ref in some if ref.shape[0] < ATT]
        whole += [jnp.concatenate(halves[at : at + 2], axis=0) for at in range(0, len(halves), 2)]
        return functools.reduce(jnp.add, whole)

    def weights(chain):
        for load in by_chain[chain]:
            load.wait()
        if chain == 0:
            every = (total(dq).T + gq[...].astype(F32)).astype(BF)
        else:
            every = total((dv, dk)[chain - 1]).astype(BF).T
        place = (0, 2, 1)[chain]
        grads[:, place * ATT : (place + 1) * ATT] = every
        if chain < 2:
            bias_sum[0:1, chain * ATT : (chain + 1) * ATT] = jnp.sum(every.astype(F32), axis=0, keepdims=True)
        made = mm(turned[...], every)
        lanes = slice(shares.lanes[chain].start, shares.lanes[chain].start + ATT)
        for owner in range(sharers):
            shares.total[owner, :, lanes] = made[owner * shard : (owner + 1) * shard]
        if chain == 1:
            extra = slice(2 * ATT, 2 * ATT + LANES)
            shares.total[:, :, extra] = jnp.zeros((sharers, shard, LANES), F32)
            for at in range(2 * ATT // LANES):
                values = bias_sum[0:1, at * LANES : (at + 1) * LANES]
                for owner in range(sharers):
                    shares.total[owner, at : at + 1, extra] = values

    def conv_grads():
        for load in others[2:]:
            load.wait()
        for copy in edge_copies():
            copy.wait()
        zero = jnp.zeros((16, ATT), F32)
        before, after = zero, zero
        if count > 1:
            before = jnp.where(block > 0, rim_in[0].astype(F32), zero)
            after = jnp.where(block < count - 1, rim_in[1].astype(F32), zero)
            nothing = jnp.zeros((16, width), BF)
            halo[0:16, :] = jnp.where(block > 0, halo_in[0], nothing)
            halo[16:32, :] = jnp.where(block < count - 1, halo_in[1], nothing)
        else:
            halo[...] = jnp.zeros_like(halo)
        lanes = slice(3 * ATT, 4 * ATT)
        grads[16 : tokens - 16, lanes] = gvalues[32:tokens, :]
        grads[0:16, lanes] = (gvalues[16:32, :].astype(F32) + before).astype(BF)
        grads[tokens - 16 : tokens, lanes] = (gvalues[tokens : tokens + 16, :].astype(F32) + after).astype(BF)

    for chain in range(chains):
        @pl.when(step == chain)
        def one(chain=chain):
            weights(chain)
            if chain == chains - 1:
                conv_grads()

    @pl.when(step >= chains)
    def by_tile():
        tile = step - chains
        first = pl.multiple_of(tile * rows, rows)
        fill_rows(window, gdepth, halo, tile, tiles, rows)
        back = mm_nt(grads[pl.ds(first, rows), :], w[...])
        for at in range(0, width, 128):
            some = slice(at, at + 128)
            depth = back[:, some] + sum_ref[:, some]
            for tap in range(KSIZE):
                depth = depth + window[20 - tap : 20 - tap + rows, some] * wide_ref[TAPS_AT + tap : TAPS_AT + tap + 1, some]
            gh_ref[:, some] = depth.astype(BF)

    def first_sends(unused):
        shares.met()
        for load in others[:2]:
            load.wait()
        for copy in edge_copies() + given_copies():
            copy.start()

    def late(eighths):
        return chains + eighths * tiles // 8

    plan = [
        (0, [(first_sends, 0), (shares.mate_start, 0)]),
        (1, [(shares.mate_end, 0), (shares.side_start, 0), (shares.mate_start, 1)]),
        (2, [(shares.mate_end, 1), (shares.side_start, 1), (shares.side_end, 0), (shares.line_start, 0), (shares.mate_start, 2)]),
        (late(0), [(shares.mate_end, 2), (shares.side_start, 2)]),
        (late(1), [(shares.side_end, 1), (shares.line_start, 1)]),
        (late(2), [(shares.line_end, 0), (shares.block_start, 0)]),
        (late(3), [(shares.side_end, 2), (shares.line_start, 2)]),
        (late(5), [(shares.line_end, 1), (shares.block_start, 1)]),
        (late(6), [(shares.line_end, 2), (shares.block_start, 2)]),
    ]
    for when in range(chains + tiles):
        actions = [action for place, some in plan if place == when for action in some]
        if actions:

            @pl.when(step == when)
            def act(actions=actions):
                for action, chain in actions:
                    action(chain)

    @pl.when(step == chains + tiles - 1)
    def end():
        for copy in given_copies():
            copy.wait()
        flat_out[...] = functools.reduce(jnp.add, [given[at].astype(F32) for at in range(count)])
        for chain in range(chains):
            sums_out[:, shares.lanes[chain]] = shares.block_end(chain)


def unpack_kernel(part, gh_ref, flat, sums, gh_out, gq_out, gk_out, gv_out, gc_out, gwd_out, gwu_out, gwn_out, gwp_out, gwk_out, gtaps_out, gkb_out, gbup_out, *refs):
    vector_outs, thin_outs = refs[:6], refs[6:10]
    shard = sums.shape[0]
    width = flat.shape[1]
    gh_out[...] = gh_ref[...]

    @pl.when(pl.program_id(0) == 0)
    def small():
        gwd_out[...] = flat[0:shard]
        quarter = shard // 2
        for group in range(2):
            for place in range(2):
                first = shard * (1 + group) + quarter * place
                gwu_out[group, :, place * width : (place + 1) * width] = flat[first : first + quarter]
            gwn_out[group] = flat[3 * shard : 5 * shard, group * ATT : (group + 1) * ATT]
        gwp_out[...] = flat[5 * shard : 6 * shard, 0:ATT]
        cells = flat[5 * shard : 6 * shard, ATT : ATT + LANES]
        turned = jnp.concatenate([cells, jnp.zeros((LANES - shard, LANES), F32)], axis=0).T
        for at, ref in enumerate(vector_outs):
            ref[...] = turned[at : at + 1, 0:shard].reshape(shard)
        gtaps_out[...] = turned[TAPS_AT : TAPS_AT + KSIZE, 0:shard]
        cells = flat[5 * shard : 6 * shard, ATT + LANES : ATT + 2 * LANES]
        gwk_out[...] = cells[0:part, 0 : HEADS * KSIZE]
        half = gbup_out.shape[0] // 2
        gbup_out[...] = jnp.concatenate(
            [cells[part : part + 1, 0:half], cells[part + 1 : part + 2, 0:half]], axis=1
        ).reshape(2 * half)
        gkb_out[...] = cells[part + 2 : part + 3, 0 : HEADS * KSIZE].reshape(HEADS * KSIZE)
        turned = jnp.concatenate([cells, jnp.zeros((LANES - shard, LANES), F32)], axis=0).T
        thin_outs[2][...] = turned[THIN_AT : THIN_AT + 1, 0:part].reshape(part)
        gq_out[...] = sums[:, 0:ATT]
        gv_out[...] = sums[:, ATT : 2 * ATT]
        gk_out[...] = sums[:, 2 * ATT + LANES :]
        gc_out[...] = flat[6 * shard : 7 * shard, 0:ATT]
        totals = jnp.concatenate(
            [sums[at : at + 1, 2 * ATT : 2 * ATT + LANES] for at in range(2 * ATT // LANES)], axis=1
        )
        lane = lax.broadcasted_iota(jnp.int32, (part, ATT), 1)
        row = lax.broadcasted_iota(jnp.int32, (part, ATT), 0)
        mine = (lane == lax.axis_index("dp") * part + row).astype(F32)
        thin_outs[3][...] = turned[THIN_AT + 1 : THIN_AT + 2, 0:part].reshape(part)
        for chain, ref in ((0, thin_outs[0]), (1, thin_outs[1])):
            picked = jnp.sum(mine * totals[:, chain * ATT : (chain + 1) * ATT], axis=1, keepdims=True)
            picked = jnp.broadcast_to(picked, (part, LANES))
            picked = jnp.concatenate([picked, jnp.zeros((LANES - part, LANES), F32)], axis=0).T
            ref[...] = picked[0:1, 0:part].reshape(part)


def unpack(grad_hidden, flat, sums, part, n_up):
    shard, width = sums.shape[0], flat.shape[1]
    shapes = [shaped((shard, ATT), F32)] * 4 + [
        shaped((shard, width), F32),
        shaped((2, shard // 2, 2 * width), F32),
        shaped((2, 2 * shard, ATT), F32),
        shaped((shard, ATT), F32),
        shaped((part, HEADS * KSIZE), F32),
        shaped((KSIZE, shard), F32),
        shaped((HEADS * KSIZE,), F32),
        shaped((n_up,), F32),
    ]
    shapes += [shaped((shard,), F32)] * 6 + [shaped((part,), F32)] * 4
    tokens = grad_hidden.shape[0]
    rows = math.gcd(tokens, 512)
    return pl.pallas_call(
        functools.partial(unpack_kernel, part),
        grid=(tokens // rows,),
        in_specs=[rows_of(rows, width), all_of(flat.shape), all_of(sums.shape)],
        out_specs=[rows_of(rows, width)] + [all_of(v.shape) for v in shapes],
        out_shape=[shaped(grad_hidden.shape, BF)] + shapes,
        compiler_params=pltpu.CompilerParams(vmem_limit_bytes=60 * MIB),
        name="unpack",
    )(grad_hidden, flat, sums)


def finish(dqs, dkvs, turned, grad_query, grad_values, grad_depth, weight, mixed, mine, wide_vectors, grad_sum, sharers, count):
    width, tokens = turned.shape
    rows = math.gcd(tokens, 256)
    tiles = tokens // rows
    blocks = len(dqs)
    chains = 3
    shard = width // sharers
    shares = Shares(sharers, shard, [ATT, ATT + LANES, ATT], [False, False, False], count)
    late_rows = pl.BlockSpec((rows, width), lambda i: (jnp.maximum(i - chains, 0), 0))
    away = pl.BlockSpec(memory_space=pl.ANY)
    loaded = list(dqs) + list(dkvs) + [turned, grad_query, grad_values, grad_depth]
    args = loaded + [weight, mixed, mine, wide_vectors, grad_sum]
    shapes = [shaped(mine.shape, F32), shaped((shard, chains * ATT + LANES), F32)]
    return pl.pallas_call(
        functools.partial(finish_kernel, blocks, rows, tiles, shares),
        grid=(chains + tiles,),
        in_specs=[away] * (len(loaded) + 2) + [all_of(mine.shape), all_of(wide_vectors.shape), late_rows],
        out_specs=[late_rows] + [all_of(v.shape) for v in shapes],
        out_shape=[shaped((tokens, width), BF)] + shapes,
        scratch_shapes=[pltpu.VMEM(v.shape, v.dtype) for v in loaded]
        + [
            pltpu.VMEM((width, 4 * ATT), BF),
            pltpu.SemaphoreType.DMA((len(loaded) + len(dkvs) + 2,)),
            pltpu.VMEM((tokens, 4 * ATT), BF),
            pltpu.VMEM((rows + 32, width), F32),
            pltpu.VMEM((8, 2 * ATT), F32),
            pltpu.VMEM((2, 16, ATT), BF),
            pltpu.VMEM((2, 16, width), BF),
            pltpu.VMEM((32, width), BF),
            pltpu.VMEM((count,) + mine.shape, BF),
            pltpu.SemaphoreType.DMA((4,)),
            pltpu.SemaphoreType.DMA((4,)),
            pltpu.SemaphoreType.DMA((max(count - 1, 1),)),
            pltpu.SemaphoreType.DMA((max(count - 1, 1),)),
        ]
        + shares.scratch(),
        compiler_params=pltpu.CompilerParams(
            collective_id=1, has_side_effects=True, vmem_limit_bytes=60 * MIB
        ),
        cost_estimate=pl.CostEstimate(
            flops=4 * tokens * width * chains * ATT, bytes_accessed=30 * tokens * width, transcendentals=0
        ),
        name="finish",
    )(*args)


def shifted_from(value, axis, step):
    count = lax.axis_size(axis)
    return lax.ppermute(value, axis, [((i + step) % count, i) for i in range(count)])


def local(
    hidden,
    separators,
    out_grad,
    w_query,
    b_query,
    w_key,
    w_value,
    b_value,
    depth_kernel,
    w_point,
    b_keyconv,
    w_kernel,
    kernel_bias,
    w_convout,
    b_convout,
    w_dense,
    b_dense,
    gain_attn,
    shift_attn,
    w_up,
    b_up,
    w_down,
    b_down,
    gain_out,
    shift_out,
):
    count = lax.axis_size("blk")
    sharers = lax.axis_size("dp")
    x, cotangent = hidden[0], out_grad[0]
    tokens, width = x.shape
    part = b_query.shape[0]

    known = math.gcd(tokens, 512) if count == 2 else 0
    others = [shifted_from(x[known:], "blk", step) for step in range(1, count)]
    weight, wide_vectors, thin, thin_columns, bias_up, wt_kernel, bias_kernel, halo, late, early = gather_columns(
        [w_query, w_key, w_value],
        [b_dense, gain_attn, shift_attn, b_down, gain_out, shift_out],
        [b_query, b_value, b_keyconv, b_convout],
        depth_kernel.T,
        b_up,
        w_kernel,
        kernel_bias,
        w_up,
        w_down,
        x,
        sharers,
        count,
    )
    mixed = jnp.concatenate([w_dense, w_convout, w_point], axis=1).astype(BF)
    mixed = lax.all_gather(mixed, "dp", axis=0, tiled=True)
    late = lax.all_gather(late, "dp", axis=0, tiled=False)

    query, query_t, *own = project([x], weight, thin, thin_columns, 3)
    keys = [own]
    outs, probs = [], []
    for step in range(count):
        if step > 0:
            keys.append(project(([early] if known else []) + [others[step - 1]], weight, thin, thin_columns, 2))
        key, key_t, value, value_t, norms = keys[step]
        out, prob = attend(separators, query_t, key, value_t, norms, count, step)
        outs.append(out)
        probs.append(prob)
        if step == 0:
            depth, keyconv, attn_key, kernt, kern, conv, values, rim = mix(
                count, x, halo, query, mixed, wide_vectors, thin, wt_kernel, bias_kernel
            )
            others, depth = lax.optimization_barrier((others, depth))
    output, grad_sum, grad_conv, grads_t, sides, (packed, g_vectors, gb_up) = middle(
        outs, conv, x, cotangent, mixed, late, wide_vectors, bias_up
    )
    grad_query_conv, grad_depth, grad_values, packed, turned = mix_back(
        count, x, halo, values, rim, grad_conv, kernt, kern, query, keyconv, attn_key, depth, mixed, wt_kernel, g_vectors, gb_up, packed
    )
    packed, sides = lax.optimization_barrier((packed, sides))
    mine = lax.psum_scatter(packed, "dp", scatter_dimension=0, tiled=False)

    dqs, dkvs = [], []
    for step in list(range(1, count)) + [0]:
        key, key_t, value, value_t, norms = keys[step]
        some = HEADS // 2 if step else HEADS
        for at in range(0, HEADS, some):
            dq, dkv = attend_back(probs[step], value, key_t, grads_t[step], sides[step], query_t, at, some)
            dqs.append(dq)
            dkvs.append(shifted_from(dkv, "blk", count - step) if step else dkv)
    grad_hidden, flat, sums = finish(
        dqs, dkvs, turned, grad_query_conv, grad_values, grad_depth, weight, mixed, mine, wide_vectors, grad_sum, sharers, count
    )
    results = unpack(grad_hidden, flat, sums, part, b_up.shape[0])
    grad_hidden, gw_query, gw_key, gw_value, gw_convout, gw_dense, gw_up, gw_down, gw_point, gw_kernel, g_taps, g_bias, gb_up = results[:13]
    g_vectors, thin = results[13:19], results[19:]
    return (
        output[None],
        grad_hidden[None],
        gw_query,
        thin[0],
        gw_key,
        gw_value,
        thin[1],
        g_taps.T,
        gw_point,
        thin[2],
        gw_kernel,
        g_bias,
        gw_convout,
        thin[3],
        gw_dense,
        g_vectors[0],
        g_vectors[1],
        g_vectors[2],
        gw_up,
        gb_up,
        gw_down,
        g_vectors[3],
        g_vectors[4],
        g_vectors[5],
    )


def solution(mesh):
    placed = (
        P("dp", "blk", None),
        P("dp"),
        P("dp", "blk", None),
        P("dp", None),
        P("dp"),
        P("dp", None),
        P("dp", None),
        P("dp"),
        P("dp", None),
        P("dp", None),
        P("dp"),
        P("dp", None),
        P(),
        P("dp", None),
        P("dp"),
        P("dp", None),
        P("dp"),
        P("dp"),
        P("dp"),
        P(None, "dp", None),
        P("dp"),
        P(None, "dp", None),
        P("dp"),
        P("dp"),
        P("dp"),
    )
    return jax.shard_map(
        local,
        mesh=mesh,
        in_specs=placed,
        out_specs=(
            P("dp", "blk", None),
            P("dp", "blk", None),
            P("dp", None),
            P("dp"),
            P("dp", None),
            P("dp", None),
            P("dp"),
            P("dp", None),
            P("dp", None),
            P("dp"),
            P("dp", None),
            P(),
            P("dp", None),
            P("dp"),
            P("dp", None),
            P("dp"),
            P("dp"),
            P("dp"),
            P(None, "dp", None),
            P("dp"),
            P(None, "dp", None),
            P("dp"),
            P("dp"),
            P("dp"),
        ),
        check_vma=False,
    )
```

profile of v0, /device:TPU:0, one launch (start us, length us, event | category | flops | bytes accessed | tf_op | source)
XLA Modules:
  0.0 435.4 jit_solution(2871512453607459658)
XLA Ops:
  7.2 0.9 convert.11
  8.1 0.9 convert.10
  9.0 0.9 convert.9
  9.9 0.7 pad_maximum_fusion
  10.6 0.0 all-gather.6.cloned.1.call-start
  10.7 30.0 %gather_columns.1 = (bf16[16,48,1408]{2,1,0:T(8,128)(2,1)}, f32[32,768]{1,0:T(8,128)}, f32[8,384]{1,0:T(8,128)}, f32[384,128]{1,0:T(8,128)}, f32[1,3072]{1,0:T(1...) custom-call(f32[48,384]{1,0:T(8,128)} %refs_0_.1, ...), custom_call_target="tpu_custom_call" | custom-call | tf_op jit(solution)/shard_map/gather_columns/pallas_call | solution.py:965
  40.8 0.0 reduce-scatter.2.cloned.1.call-start
  40.8 1.6 slice_bitcast_fusion
  42.4 1.5 collective-permute-start
  44.5 12.2 %project.2 = (bf16[2048,384]{1,0:T(8,128)(2,1)}, bf16[384,2048]{1,0:T(8,128)(2,1)}, bf16[2048,384]{1,0:T(8,128)(2,1)}, bf16[384,2048]{1,0:T(8,128)(2,1)}, bf16[2...) custom-call(bf16[2048,768]{1,0:T(8,128)(2,1)} %bitcast.14, bf16[768,1408]{1,0:T(8,128)(2,1)} %bitcast.18, ...), custom_call_target="tpu_custom_call" | custom-call | flops 7247757312 | bytes 14970880 | tf_op jit(solution)/shard_map/project/pallas_call | solution.py:232
  56.7 42.7 %attend.2 = (f32[6,80,2048]{2,1,0:T(8,128)}, bf16[6,2048,2048]{2,1,0:T(8,128)(2,1)}) custom-call(s32[1]{0:T(128)S(6)} %copy.51.at_ref, bf16[384,2048]{1,0:T(8,128)(2,1)} %get-tuple-element.113.q_ref, bf16[2048,384]{1,0:T(8,128)(2,1)} %get-tuple-element.114.k_ref, bf16[384,2048]{1,0:T(8,128)(2,1)} %get-tuple-element.115.v_ref, ...), custom_call_target="tpu_custom_call" | custom-call | flops 786432 | bytes 24576 | tf_op jit(solution)/shard_map/attend/pallas_call | solution.py:115
  99.4 22.0 %mix.1 = (bf16[2048,768]{1,0:T(8,128)(2,1)}, f32[2048,384]{1,0:T(8,128)}, bf16[2048,384]{1,0:T(8,128)(2,1)}, f32[72,2048]{1,0:T(8,128)}, bf16[2048,128]{1,0:T(8,...) custom-call(bf16[2048,768]{1,0:T(8,128)(2,1)} %bitcast.15, ...), custom_call_target="tpu_custom_call" | custom-call | flops 9663676416 | bytes 21837824 | tf_op jit(solution)/shard_map/mix/pallas_call | solution.py:232
  121.4 9.2 %project.3 = (bf16[2048,384]{1,0:T(8,128)(2,1)}, bf16[384,2048]{1,0:T(8,128)(2,1)}, bf16[2048,384]{1,0:T(8,128)(2,1)}, bf16[384,2048]{1,0:T(8,128)(2,1)}, f32[8,512]{1,0:T(8,128)}) custom-call(bf16[512,768]{1,0:T(8,128)(2,1)} %get-tuple-element.118.refs_0_, bf16[1536,768]{1,0:T(8,128)(2,1)} %collective-permute-done.refs_1_, bf16[768,1408]{1,0:T(8,128)(2,1)} %bitcast.19, ...), custom_call_target="tpu_custom_call" | custom-call | flops 4831838208 | bytes 11825152 | tf_op jit(solution)/shard_map/project/pallas_call | solution.py:232
  130.7 35.7 %attend.3 = (f32[6,80,2048]{2,1,0:T(8,128)}, bf16[6,2048,2048]{2,1,0:T(8,128)(2,1)}) custom-call(s32[1]{0:T(128)S(6)} %copy.51.at_ref, bf16[384,2048]{1,0:T(8,128)(2,1)} %get-tuple-element.113.q_ref, bf16[2048,384]{1,0:T(8,128)(2,1)} %get-tuple-element.126.k_ref, bf16[384,2048]{1,0:T(8,128)(2,1)} %get-tuple-element.127.v_ref, ...), custom_call_target="tpu_custom_call" | custom-call | flops 786432 | bytes 24576 | tf_op jit(solution)/shard_map/attend/pallas_call | solution.py:115
  166.4 74.7 %middle.1 = (bf16[2048,768]{1,0:T(8,128)(2,1)}, f32[2048,768]{1,0:T(8,128)}, bf16[2048,384]{1,0:T(8,128)(2,1)}, bf16[384,2048]{1,0:T(8,128)(2,1)}, bf16[384,2048...) custom-call(f32[6,80,2048]{2,1,0:T(8,128)} %get-tuple-element.117.re, ...), custom_call_target="tpu_custom_call" | custom-call | flops 36238786560 | bytes 46239744 | tf_op jit(solution)/shard_map/middle/pallas_call | solution.py:232
  241.1 32.3 %mix_back.1 = (bf16[2048,384]{1,0:T(8,128)(2,1)}, bf16[2048,768]{1,0:T(8,128)(2,1)}, bf16[2080,384]{1,0:T(8,128)(2,1)}, bf16[16,336,768]{2,1,0:T(8,128)(2,1)}, bf16[768,2048]{1,0:T(8,128)(2,1)}) custom-call(bf16[2048,768]{1,0:T(8,128)(2,1)} %bitcast.17, bf16[32,768]{1,0:T(8,128)(2,1)} %get-tuple-element.119.halo_ref, ...), custom_call_target="tpu_custom_call", output_to_operand_aliasing={{3}: (15, {})} | custom-call | flops 9663676416 | bytes 45430784 | tf_op jit(solution)/shard_map/mix_back/pallas_call | solution.py:232
  273.4 27.8 %attend_back.4 = (bf16[192,2048]{1,0:T(8,128)(2,1)}, bf16[2,192,2048]{2,1,0:T(8,128)(2,1)}) custom-call(bf16[6,2048,2048]{2,1,0:T(8,128)(2,1)} %get-tuple-element.134.p_ref, bf16[2048,384]{1,0:T(8,128)(2,1)} %get-tuple-element.135.v_ref, bf16[384,2048]{1,0:T(8,128)(2,1)} %get-tuple-element.136.kt_ref, bf16[384,2048]{1,0:T(8,128)(2,1)} %get-tuple-element.137.g_ref, ...), custom_call_target="tpu_custom_call" | custom-call | flops 25769803776 | bytes 25165824 | tf_op jit(solution)/shard_map/attend_back/pallas_call | solution.py:181
  301.2 28.1 %attend_back.3 = (bf16[192,2048]{1,0:T(8,128)(2,1)}, bf16[2,192,2048]{2,1,0:T(8,128)(2,1)}) custom-call(bf16[6,2048,2048]{2,1,0:T(8,128)(2,1)} %get-tuple-element.134.p_ref, bf16[2048,384]{1,0:T(8,128)(2,1)} %get-tuple-element.135.v_ref, bf16[384,2048]{1,0:T(8,128)(2,1)} %get-tuple-element.136.kt_ref, bf16[384,2048]{1,0:T(8,128)(2,1)} %get-tuple-element.137.g_ref, ...), custom_call_target="tpu_custom_call" | custom-call | flops 25769803776 | bytes 25165824 | tf_op jit(solution)/shard_map/attend_back/pallas_call | solution.py:181
  329.3 2.0 collective-permute-start.1
  331.3 52.0 %attend_back.5 = (bf16[384,2048]{1,0:T(8,128)(2,1)}, bf16[2,384,2048]{2,1,0:T(8,128)(2,1)}) custom-call(bf16[6,2048,2048]{2,1,0:T(8,128)(2,1)} %get-tuple-element.155.p_ref, bf16[2048,384]{1,0:T(8,128)(2,1)} %get-tuple-element.156.v_ref, bf16[384,2048]{1,0:T(8,128)(2,1)} %get-tuple-element.157.kt_ref, bf16[384,2048]{1,0:T(8,128)(2,1)} %get-tuple-element.158.g_ref, ...), custom_call_target="tpu_custom_call" | custom-call | flops 51539607552 | bytes 50331648 | tf_op jit(solution)/shard_map/attend_back/pallas_call | solution.py:181
  383.3 1.1 copy-done.1
  384.4 0.5 copy-done.2
  384.9 38.5 %finish.1 = (bf16[2048,768]{1,0:T(8,128)(2,1)}, f32[336,768]{1,0:T(8,128)}, f32[48,1280]{1,0:T(8,128)}) custom-call(bf16[192,2048]{1,0:T(8,128)(2,1)} %get-tuple-element.153.refs_0_, bf16[192,2048]{1,0:T(8,128)(2,1)} %get-tuple-element.154.refs_1_, bf16[384,2048]{1,0:T(8,128)(2,1)} %get-tuple-element.160.refs_2_, bf16[2,192,2048]{2,1,0:T(8,128)(2,1)} %copy-done.2, ...), custom_call_target="tpu_custom_call" | custom-call | flops 7247757312 | bytes 47185920 | tf_op jit(solution)/shard_map/finish/pallas_call | solution.py:1385
  423.4 5.2 %unpack.1 = (bf16[2048,768]{1,0:T(8,128)(2,1)}, f32[48,384]{1,0:T(8,128)}, f32[48,384]{1,0:T(8,128)}, f32[48,384]{1,0:T(8,128)}, f32[48,384]{1,0:T(8,128)}, /*in...) custom-call(bf16[2048,768]{1,0:T(8,128)(2,1)} %get-tuple-element.170, ...), custom_call_target="tpu_custom_call" | custom-call | tf_op jit(solution)/shard_map/unpack/pallas_call | solution.py:1361
  (15 shorter events, 0.1 us)
Async XLA Ops:
  7.2 92.2 %all-gather.4.cloned.1.call-start = ((), (), s32[]{:S(2)}) async-start(), calls=%async_computation.1 | async-start | bytes 2506752 | tf_op jit(solution)/shard_map/all_gather | solution.py:1473
  10.6 155.7 %all-gather.6.cloned.1.call-start = ((), (), s32[]{:S(2)}) async-start(), calls=%async_computation.3 | async-start | bytes 5013504 | tf_op jit(solution)/shard_map/all_gather | solution.py:1474
  10.7 30.1 %copy-start = (bf16[1,2048,768]{2,1,0:T(8,128)(2,1)S(1)}, bf16[1,2048,768]{2,1,0:T(8,128)(2,1)}, u32[]{:S(2)}) copy-start(bf16[1,2048,768]{2,1,0:T(8,128)(2,1)} %param.25) | copy-start | bytes 9437188
  40.8 342.6 %reduce-scatter.2.cloned.1.call-start = ((), (), s32[]{:S(2)}) async-start(), calls=%async_computation.2 | async-start | bytes 8773632 | tf_op jit(solution)/shard_map/reduce_scatter | solution.py:1498
  42.4 79.1 %collective-permute-start = (bf16[1536,768]{1,0:T(8,128)(2,1)}, bf16[1536,768]{1,0:T(8,128)(2,1)}, u32[]{:S(2)}, u32[]{:S(2)}) collective-permute-start(bf16[1536,768]{1,0:T(8,128)(2,1)} %slice_bitcast_fusion), channel_id=1, source_target_pairs={{16,0},{0,16},{17,1},{1,17},{18,2},{2,18},{19,3},{3,19},{20,4},{4,... | collective-permute-start | bytes 7077896 | tf_op jit(solution)/shard_map/ppermute | solution.py:1420
  301.2 82.1 %collective-permute-start.2 = (bf16[2,192,2048]{2,1,0:T(8,128)(2,1)}, bf16[2,192,2048]{2,1,0:T(8,128)(2,1)S(1)}, u32[]{:S(2)}, u32[]{:S(2)}) collective-permute-start(bf16[2,192,2048]{2,1,0:T(8,128)(2,1)} %get-tuple-element.162), channel_id=1, source_target_pairs={{16,0},{0,16},{17,1},{1,17},{18,2},{2,18},{19,3},{3,19},{20,4},{4,... | collective-permute-start | bytes 4718600 | tf_op jit(solution)/shard_map/ppermute | solution.py:1420
  329.3 54.0 %collective-permute-start.1 = (bf16[2,192,2048]{2,1,0:T(8,128)(2,1)}, bf16[2,192,2048]{2,1,0:T(8,128)(2,1)S(1)}, u32[]{:S(2)}, u32[]{:S(2)}) collective-permute-start(bf16[2,192,2048]{2,1,0:T(8,128)(2,1)} %get-tuple-element.161), channel_id=1, source_target_pairs={{16,0},{0,16},{17,1},{1,17},{18,2},{2,18},{19,3},{3,19},{20,4},{4,... | collective-permute-start | bytes 4718600 | tf_op jit(solution)/shard_map/ppermute | solution.py:1420
  383.3 1.1 copy-start.1
  383.3 1.6 copy-start.2
Sparse Core Ops, SparseCore 0:
  10.9 45.5 all-gather.3
  58.7 52.2 all-gather.5
  273.5 109.1 reduce-scatter.1
where the time goes:
time: 444 us; the launch traced here: 435 us
  Pallas kernels  410 us (92%)
  between operations  14.7 us (3%)
    pallas_call x5, Pallas kernels, run_tiles(): pl.pallas_call(kernel, grid=(steps,), in_specs=list(in_specs), out_specs=...  150 us
    pallas_call x3, Pallas kernels, attend_back(): pl.pallas_call(functools.partial(attend_back_kernel, first, keys, queries...  108 us
    pallas_call x2, Pallas kernels, attend(): pl.pallas_call(functools.partial(attend_kernel, keys, queries, chunk, cou...  78.4 us
    pallas_call x1, Pallas kernels, finish(): pl.pallas_call(functools.partial(finish_kernel, blocks, rows, tiles, shar...  38.5 us
    pallas_call x1, Pallas kernels, gather_columns(): pl.pallas_call(functools.partial(gather_kernel, sharers, count, part, ear...  30 us
  transfers between devices with their start and end apart: 6, of which 0 were waited for; matrix products, arithmetic and copies ran while one was open for 0% of the time, Pallas kernels for 60%

commit v1 on v0

--- a/solution.py
+++ b/solution.py
@@ -249,28 +249,27 @@
 
 def project_kernel(parts, sources, *refs):
     x_refs, refs = refs[:sources], refs[sources:]
-    (w_ref, thin_ref, thin_columns_ref), refs = refs[:3], refs[3:]
-    norm_ref, flipped = refs[2 * parts], refs[2 * parts + 1]
+    (w_ref, thin_ref), refs = refs[:2], refs[2:]
+    norm_ref = refs[2 * parts]
     skip = (3 - parts) * ATT
 
     @pl.when(pl.program_id(0) == 0)
     def start():
         norm_ref[...] = jnp.zeros_like(norm_ref)
-        flipped[...] = w_ref[:, skip:].T
 
     x = x_refs[-1][...]
     if sources == 2:
         x = jnp.where(pl.program_id(0) == 0, x_refs[0][...], x)
     plain = mm(x, w_ref[:, skip:])
-    turned = mm_nt(flipped[...], x)
     for part in range(parts):
         own = slice(part * ATT, (part + 1) * ATT)
-        bias, bias_t = 0.0, 0.0
+        bias = 0.0
         if part != parts - 2:
             at = 1 if part == parts - 1 else 0
-            bias, bias_t = thin_ref[at : at + 1, :], thin_columns_ref[:, THIN_AT + at : THIN_AT + at + 1]
-        refs[2 * part][...] = (plain[:, own] + bias).astype(BF)
-        across = (turned[own] + bias_t).astype(BF)
+            bias = thin_ref[at : at + 1, :]
+        low = (plain[:, own] + bias).astype(BF)
+        refs[2 * part][...] = low
+        across = low.T
         if part == parts - 2:
             wide = across.astype(F32)
             for head in range(HEADS):
@@ -282,7 +281,7 @@
         refs[2 * part + 1][...] = across
 
 
-def project(sources, weight, thin, thin_columns, parts):
+def project(sources, weight, thin, parts):
     tokens, width = sum(x.shape[0] for x in sources), sources[0].shape[1]
     wide = 3 * ATT
     tile = math.gcd(tokens, 512)
@@ -303,11 +302,10 @@
         + [
             (weight, all_of((width, wide))),
             (thin, all_of(thin.shape)),
-            (thin_columns, all_of(thin_columns.shape)),
         ],
         outputs,
-        [pltpu.VMEM((parts * ATT, width), BF)],
-        4 * tokens * width * parts * ATT,
+        [],
+        2 * tokens * width * parts * ATT,
     )
 
 
@@ -381,10 +379,13 @@
     kernt_ref[...] = kernt[0 : 8 * KSIZE]
     kern = kernt.astype(BF).T
     kern_ref[...] = kern
-    total = jnp.zeros((rows, ATT), F32)
-    for tap in range(KSIZE):
-        total = total + mm(kern, spread[:, tap * ATT : (tap + 1) * ATT]) * conv_window[12 + tap : 12 + tap + rows, :]
-    conv_ref[...] = total.astype(BF)
+    for at in range(0, ATT, LANES):
+        some = slice(at, at + LANES)
+        total = jnp.zeros((rows, LANES), F32)
+        for tap in range(KSIZE):
+            first = tap * ATT + at
+            total = total + mm(kern, spread[:, first : first + LANES]) * conv_window[12 + tap : 12 + tap + rows, some]
+        conv_ref[:, some] = total.astype(BF)
 
 
 def column_block(weight, place):
@@ -451,9 +452,14 @@
     (out_ref, sum_ref, gconv_ref), refs = refs[:3], refs[3:]
     g_refs, refs = refs[:blocks], refs[blocks:]
     side_refs, refs = refs[:blocks], refs[blocks:]
-    (packed_ref, gvec_ref, gbu_ref, wd_sum, wu_sum, wn_sum, acts, slopes, staged, sems, wu_ref, wn_ref) = refs
+    (packed_ref, gvec_ref, gbu_ref, wd_sum, wu_sum, wn_sum, acts, slopes, staged, sems, wu_ref) = refs
     tile = pl.program_id(0)
     hidden_units = wu_ref.shape[1]
+    low_rows = late_ref.shape[1] // 2
+
+    def down_rows(at, lanes):
+        return late_ref[at // low_rows : (at + units) // low_rows, low_rows:, lanes].reshape(units, ATT)
+
     groups = 2
     inner = ATT
     outer = hidden_units // groups
@@ -471,8 +477,6 @@
                 wu_ref[pair * quarter : (pair + 2) * quarter, place * width : (place + 1) * width] = (
                     jnp.concatenate(some, axis=0).astype(BF)
                 )
-        for owner in range(owners):
-            wn_ref[owner * high // 2 : (owner + 1) * high // 2] = late_ref[owner, high // 2 :]
 
     shifts = [ref[:, HD + 8 : HD + 9, :] for ref in o_refs]
     top = functools.reduce(jnp.maximum, shifts)
@@ -498,7 +502,7 @@
             act = act.astype(BF)
             acts[:, here] = act
             slopes[:, here] = slope.astype(BF)
-            down = down + mm(act, wn_ref[at : at + units, group * inner : (group + 1) * inner])
+            down = down + mm(act, down_rows(at, slice(group * inner, (group + 1) * inner)))
         downs.append(down)
     unit_two, scale_two = normal(jnp.concatenate(downs, axis=1) + vec[3] + normed)
     out_ref[...] = (unit_two * vec[4] + vec[5]).astype(BF)
@@ -516,7 +520,7 @@
         back = jnp.zeros((rows, inner), F32)
         for at in range(0, outer, units):
             here = slice(group * outer + at, group * outer + at + units)
-            grad_act = mm_nt(grads, wn_ref[at : at + units, lanes])
+            grad_act = mm_nt(grads, down_rows(at, lanes))
             grad_up = (grad_act * slopes[:, here].astype(F32)).astype(BF)
             gbu_ref[0:1, here] += jnp.sum(grad_up.astype(F32), axis=0, keepdims=True)
             wn_sum[at : at + units, lanes] += mm_tn(acts[:, here], grads)
@@ -620,7 +624,6 @@
             pltpu.VMEM((2, 5 * shard, width), BF),
             pltpu.SemaphoreType.DMA((sharers,)),
             pltpu.VMEM(up, BF),
-            pltpu.VMEM(down, BF),
         ],
         6 * tokens * (width * width + 2 * math.prod(up)),
     )
@@ -772,6 +775,20 @@
     )
 
 
+def side_by_side_kernel(*refs):
+    at = 0
+    for ref in refs[:-1]:
+        refs[-1][:, at : at + ref.shape[1]] = ref[...].astype(BF)
+        at += ref.shape[1]
+
+
+def side_by_side(parts):
+    out = shaped((parts[0].shape[0], sum(v.shape[1] for v in parts)), BF)
+    return run_tiles(
+        side_by_side_kernel, "side_by_side", 1, [(v, all_of(v.shape)) for v in parts], [(out, all_of(out.shape))], [], 0
+    )[0]
+
+
 MESH = pl.DeviceIdType.MESH
 LINE = 4
 LANES = 128
@@ -809,7 +826,7 @@
     vector_refs, refs = refs[:6], refs[6:]
     thin_refs, refs = refs[:4], refs[4:]
     (taps_ref, up_ref, kernel_ref, bias_ref, wu_ref, wn_ref, head_ref, tail_ref, early_ref), refs = refs[:9], refs[9:]
-    (out_ref, wide_ref, thin_ref, thin_columns_ref, bias_up_ref, wk_ref, bk_ref, halo_ref, late_out, early_out), refs = refs[:10], refs[10:]
+    (out_ref, wide_ref, thin_ref, bias_up_ref, wk_ref, bk_ref, halo_ref, late_out, early_out), refs = refs[:9], refs[9:]
     rows, side, flat, thin_flat, edges, send_sem, recv_sem, edge_send, edge_recv = refs
     me, line, column, core, columns = my_place(sharers)
     block = lax.axis_index("blk")
@@ -925,7 +942,6 @@
         thin_flat[owner * part : (owner + 1) * part, :] = cells[0:part]
     turned = flat[...].T
     wide_ref[...] = turned[0 : wide_ref.shape[0]]
-    thin_columns_ref[...] = thin_flat[...]
     thin_ref[...] = thin_flat[...].T[THIN_AT : THIN_AT + 8]
     for owner in range(sharers):
         cells = out_ref[owner, :, base + LANES :].astype(F32)
@@ -954,7 +970,6 @@
         shaped((sharers, shard, wide), BF),
         shaped((32, width), F32),
         shaped((8, ATT), F32),
-        shaped((ATT, LANES), F32),
         shaped((1, sharers * b_up.shape[0]), F32),
         shaped((8 * KSIZE, ATT), BF),
         shaped((8 * KSIZE, LANES), F32),
@@ -1197,7 +1212,7 @@
         for load in by_chain[chain]:
             load.wait()
         if chain == 0:
-            every = (total(dq).T + gq[...].astype(F32)).astype(BF)
+            every = (total(dq).astype(BF).T.astype(F32) + gq[...].astype(F32)).astype(BF)
         else:
             every = total((dv, dk)[chain - 1]).astype(BF).T
         place = (0, 2, 1)[chain]
@@ -1357,7 +1372,7 @@
     ]
     shapes += [shaped((shard,), F32)] * 6 + [shaped((part,), F32)] * 4
     tokens = grad_hidden.shape[0]
-    rows = math.gcd(tokens, 512)
+    rows = math.gcd(tokens, 1024)
     return pl.pallas_call(
         functools.partial(unpack_kernel, part),
         grid=(tokens // rows,),
@@ -1406,7 +1421,7 @@
         ]
         + shares.scratch(),
         compiler_params=pltpu.CompilerParams(
-            collective_id=1, has_side_effects=True, vmem_limit_bytes=60 * MIB
+            collective_id=1, has_side_effects=True, vmem_limit_bytes=62 * MIB
         ),
         cost_estimate=pl.CostEstimate(
             flops=4 * tokens * width * chains * ATT, bytes_accessed=30 * tokens * width, transcendentals=0
@@ -1455,7 +1470,7 @@
 
     known = math.gcd(tokens, 512) if count == 2 else 0
     others = [shifted_from(x[known:], "blk", step) for step in range(1, count)]
-    weight, wide_vectors, thin, thin_columns, bias_up, wt_kernel, bias_kernel, halo, late, early = gather_columns(
+    weight, wide_vectors, thin, bias_up, wt_kernel, bias_kernel, halo, late, early = gather_columns(
         [w_query, w_key, w_value],
         [b_dense, gain_attn, shift_attn, b_down, gain_out, shift_out],
         [b_query, b_value, b_keyconv, b_convout],
@@ -1469,16 +1484,15 @@
         sharers,
         count,
     )
-    mixed = jnp.concatenate([w_dense, w_convout, w_point], axis=1).astype(BF)
-    mixed = lax.all_gather(mixed, "dp", axis=0, tiled=True)
+    mixed = lax.all_gather(side_by_side([w_dense, w_convout, w_point]), "dp", axis=0, tiled=True)
     late = lax.all_gather(late, "dp", axis=0, tiled=False)
 
-    query, query_t, *own = project([x], weight, thin, thin_columns, 3)
+    query, query_t, *own = project([x], weight, thin, 3)
     keys = [own]
     outs, probs = [], []
     for step in range(count):
         if step > 0:
-            keys.append(project(([early] if known else []) + [others[step - 1]], weight, thin, thin_columns, 2))
+            keys.append(project(([early] if known else []) + [others[step - 1]], weight, thin, 2))
         key, key_t, value, value_t, norms = keys[step]
         out, prob = attend(separators, query_t, key, value_t, norms, count, step)
         outs.append(out)

time: 444 us -> 423 us (0.953); the launches traced: 435 us -> 421 us
  Pallas kernels: 410 us -> 383 us
  waiting for transfers between devices: 0.08 us -> 18.8 us
    pallas_call x2, Pallas kernels: 78.4 us -> 57 us  [attend(): pl.pallas_call(functools.partial(attend_kernel, keys, queries, chunk, cou...]
    reduce_scatter x1, waiting for transfers between devices: 0.02 us -> 18.8 us  [local(): mine = lax.psum_scatter(packed, 'dp', scatter_dimension=0, tiled=False)]
    pallas_call x5 -> x6, Pallas kernels: 150 us -> 145 us  [run_tiles(): pl.pallas_call(kernel, grid=(steps,), in_specs=list(in_specs), out_specs=...]
  transfers between devices with their start and end apart: 6 -> 6, of which waited for: 0 -> 1; matrix products, arithmetic and copies ran while one was open for 0% -> 0% of each run, Pallas kernels for 60% -> 55%
where the time goes in v1:
time: 423 us; the launch traced here: 421 us
  Pallas kernels  383 us (91%)
  waiting for transfers between devices  18.8 us (4%)
  between operations  15 us (4%)
    pallas_call x6, Pallas kernels, run_tiles(): pl.pallas_call(kernel, grid=(steps,), in_specs=list(in_specs), out_specs=...  145 us
    pallas_call x3, Pallas kernels, attend_back(): pl.pallas_call(functools.partial(attend_back_kernel, first, keys, queries...  108 us
    pallas_call x2, Pallas kernels, attend(): pl.pallas_call(functools.partial(attend_kernel, keys, queries, chunk, cou...  57 us
    pallas_call x1, Pallas kernels, finish(): pl.pallas_call(functools.partial(finish_kernel, blocks, rows, tiles, shar...  39.8 us
    pallas_call x1, Pallas kernels, gather_columns(): pl.pallas_call(functools.partial(gather_kernel, sharers, count, part, ear...  28.9 us
    reduce_scatter x1, waiting for transfers between devices, local(): mine = lax.psum_scatter(packed, 'dp', scatter_dimension=0, tiled=False)  18.8 us
  transfers between devices with their start and end apart: 6, of which 1 were waited for; matrix products, arithmetic and copies ran while one was open for 0% of the time, Pallas kernels for 55%

profile of v1, /device:TPU:0, one launch (start us, length us, event | category | flops | bytes accessed | tf_op | source)
XLA Modules:
  0.0 421.4 jit_solution(3672885906846887110)
XLA Ops:
  7.2 0.0 all-gather.4.cloned.1.call-start
  7.2 1.7 side_by_side.1
  8.9 0.0 all-gather.6.cloned.1.call-start
  9.0 28.9 %gather_columns.1 = (bf16[16,48,1408]{2,1,0:T(8,128)(2,1)}, f32[32,768]{1,0:T(8,128)}, f32[8,384]{1,0:T(8,128)}, f32[1,3072]{1,0:T(1,128)}, bf16[72,384]{1,0:T(8...) custom-call(f32[48,384]{1,0:T(8,128)} %refs_0_.2, ...), custom_call_target="tpu_custom_call" | custom-call | tf_op jit(solution)/shard_map/gather_columns/pallas_call | solution.py:980
  37.9 0.0 all-gather.6.cloned.1.call-update
  37.9 0.0 reduce-scatter.2.cloned.1.call-start
  38.0 1.6 slice_bitcast_fusion
  39.6 0.6 collective-permute-start
  40.8 8.6 %project.2 = (bf16[2048,384]{1,0:T(8,128)(2,1)}, bf16[384,2048]{1,0:T(8,128)(2,1)}, bf16[2048,384]{1,0:T(8,128)(2,1)}, bf16[384,2048]{1,0:T(8,128)(2,1)}, bf16[2...) custom-call(bf16[2048,768]{1,0:T(8,128)(2,1)} %bitcast.14, bf16[768,1408]{1,0:T(8,128)(2,1)} %bitcast.18, ...), custom_call_target="tpu_custom_call" | custom-call | flops 3623878656 | bytes 14774272 | tf_op jit(solution)/shard_map/project/pallas_call | solution.py:232
  49.4 28.5 %attend.2 = (f32[6,80,2048]{2,1,0:T(8,128)}, bf16[6,2048,2048]{2,1,0:T(8,128)(2,1)}) custom-call(s32[1]{0:T(128)S(6)} %copy.51.at_ref, bf16[384,2048]{1,0:T(8,128)(2,1)} %get-tuple-element.111.q_ref, bf16[2048,384]{1,0:T(8,128)(2,1)} %get-tuple-element.112.k_ref, bf16[384,2048]{1,0:T(8,128)(2,1)} %get-tuple-element.113.v_ref, ...), custom_call_target="tpu_custom_call" | custom-call | flops 786432 | bytes 24576 | tf_op jit(solution)/shard_map/attend/pallas_call | solution.py:115
  77.9 20.7 %mix.1 = (bf16[2048,768]{1,0:T(8,128)(2,1)}, f32[2048,384]{1,0:T(8,128)}, bf16[2048,384]{1,0:T(8,128)(2,1)}, f32[72,2048]{1,0:T(8,128)}, bf16[2048,128]{1,0:T(8,...) custom-call(bf16[2048,768]{1,0:T(8,128)(2,1)} %bitcast.15, ...), custom_call_target="tpu_custom_call" | custom-call | flops 9663676416 | bytes 21837824 | tf_op jit(solution)/shard_map/mix/pallas_call | solution.py:232
  98.6 7.8 %project.3 = (bf16[2048,384]{1,0:T(8,128)(2,1)}, bf16[384,2048]{1,0:T(8,128)(2,1)}, bf16[2048,384]{1,0:T(8,128)(2,1)}, bf16[384,2048]{1,0:T(8,128)(2,1)}, f32[8,512]{1,0:T(8,128)}) custom-call(bf16[512,768]{1,0:T(8,128)(2,1)} %get-tuple-element.116.refs_0_, bf16[1536,768]{1,0:T(8,128)(2,1)} %collective-permute-done.refs_1_, bf16[768,1408]{1,0:T(8,128)(2,1)} %bitcast.19, ...), custom_call_target="tpu_custom_call" | custom-call | flops 2415919104 | bytes 11628544 | tf_op jit(solution)/shard_map/project/pallas_call | solution.py:232
  106.3 28.6 %attend.3 = (f32[6,80,2048]{2,1,0:T(8,128)}, bf16[6,2048,2048]{2,1,0:T(8,128)(2,1)}) custom-call(s32[1]{0:T(128)S(6)} %copy.51.at_ref, bf16[384,2048]{1,0:T(8,128)(2,1)} %get-tuple-element.111.q_ref, bf16[2048,384]{1,0:T(8,128)(2,1)} %get-tuple-element.124.k_ref, bf16[384,2048]{1,0:T(8,128)(2,1)} %get-tuple-element.125.v_ref, ...), custom_call_target="tpu_custom_call" | custom-call | flops 786432 | bytes 24576 | tf_op jit(solution)/shard_map/attend/pallas_call | solution.py:115
  134.9 74.3 %middle.1 = (bf16[2048,768]{1,0:T(8,128)(2,1)}, f32[2048,768]{1,0:T(8,128)}, bf16[2048,384]{1,0:T(8,128)(2,1)}, bf16[384,2048]{1,0:T(8,128)(2,1)}, bf16[384,2048...) custom-call(f32[6,80,2048]{2,1,0:T(8,128)} %get-tuple-element.115.re, ...), custom_call_target="tpu_custom_call" | custom-call | flops 36238786560 | bytes 46239744 | tf_op jit(solution)/shard_map/middle/pallas_call | solution.py:232
  209.3 32.4 %mix_back.1 = (bf16[2048,384]{1,0:T(8,128)(2,1)}, bf16[2048,768]{1,0:T(8,128)(2,1)}, bf16[2080,384]{1,0:T(8,128)(2,1)}, bf16[16,336,768]{2,1,0:T(8,128)(2,1)}, bf16[768,2048]{1,0:T(8,128)(2,1)}) custom-call(bf16[2048,768]{1,0:T(8,128)(2,1)} %bitcast.17, bf16[32,768]{1,0:T(8,128)(2,1)} %get-tuple-element.117.halo_ref, ...), custom_call_target="tpu_custom_call", output_to_operand_aliasing={{3}: (15, {})} | custom-call | flops 9663676416 | bytes 45430784 | tf_op jit(solution)/shard_map/mix_back/pallas_call | solution.py:232
  241.6 0.0 reduce-scatter.2.cloned.1.call-update
  241.7 27.8 %attend_back.4 = (bf16[192,2048]{1,0:T(8,128)(2,1)}, bf16[2,192,2048]{2,1,0:T(8,128)(2,1)}) custom-call(bf16[6,2048,2048]{2,1,0:T(8,128)(2,1)} %get-tuple-element.132.p_ref, bf16[2048,384]{1,0:T(8,128)(2,1)} %get-tuple-element.133.v_ref, bf16[384,2048]{1,0:T(8,128)(2,1)} %get-tuple-element.134.kt_ref, bf16[384,2048]{1,0:T(8,128)(2,1)} %get-tuple-element.135.g_ref, ...), custom_call_target="tpu_custom_call" | custom-call | flops 25769803776 | bytes 25165824 | tf_op jit(solution)/shard_map/attend_back/pallas_call | solution.py:181
  269.4 1.4 collective-permute-start.2
  270.9 28.1 %attend_back.3 = (bf16[192,2048]{1,0:T(8,128)(2,1)}, bf16[2,192,2048]{2,1,0:T(8,128)(2,1)}) custom-call(bf16[6,2048,2048]{2,1,0:T(8,128)(2,1)} %get-tuple-element.132.p_ref, bf16[2048,384]{1,0:T(8,128)(2,1)} %get-tuple-element.133.v_ref, bf16[384,2048]{1,0:T(8,128)(2,1)} %get-tuple-element.134.kt_ref, bf16[384,2048]{1,0:T(8,128)(2,1)} %get-tuple-element.135.g_ref, ...), custom_call_target="tpu_custom_call" | custom-call | flops 25769803776 | bytes 25165824 | tf_op jit(solution)/shard_map/attend_back/pallas_call | solution.py:181
  299.0 0.6 collective-permute-start.1
  299.6 52.0 %attend_back.5 = (bf16[384,2048]{1,0:T(8,128)(2,1)}, bf16[2,384,2048]{2,1,0:T(8,128)(2,1)}) custom-call(bf16[6,2048,2048]{2,1,0:T(8,128)(2,1)} %get-tuple-element.153.p_ref, bf16[2048,384]{1,0:T(8,128)(2,1)} %get-tuple-element.154.v_ref, bf16[384,2048]{1,0:T(8,128)(2,1)} %get-tuple-element.155.kt_ref, bf16[384,2048]{1,0:T(8,128)(2,1)} %get-tuple-element.156.g_ref, ...), custom_call_target="tpu_custom_call" | custom-call | flops 51539607552 | bytes 50331648 | tf_op jit(solution)/shard_map/attend_back/pallas_call | solution.py:181
  351.6 18.8 %reduce-scatter.2.cloned.1.call-done = bf16[1,336,768]{2,1,0:T(8,128)(2,1)} async-done(((bf16[16,336,768]{2,1,0:T(8,128)(2,1)}), bf16[1,336,768]{2,1,0:T(8,128)(2,1)}) %reduce-scatter.2.cloned.1.call-update) | async-done | bytes 516112 | tf_op jit(solution)/shard_map/reduce_scatter | solution.py:1512
  370.4 39.8 %finish.1 = (bf16[2048,768]{1,0:T(8,128)(2,1)}, f32[336,768]{1,0:T(8,128)}, f32[48,1280]{1,0:T(8,128)}) custom-call(bf16[192,2048]{1,0:T(8,128)(2,1)} %get-tuple-element.151.refs_0_, bf16[192,2048]{1,0:T(8,128)(2,1)} %get-tuple-element.152.refs_1_, bf16[384,2048]{1,0:T(8,128)(2,1)} %get-tuple-element.158.refs_2_, ...), custom_call_target="tpu_custom_call" | custom-call | flops 7247757312 | bytes 47185920 | tf_op jit(solution)/shard_map/finish/pallas_call | solution.py:1400
  410.2 4.2 unpack.1
  (10 shorter events, 0.0 us)
Async XLA Ops:
  7.2 70.7 %all-gather.4.cloned.1.call-start = ((), (), s32[]{:S(2)}) async-start(), calls=%async_computation.1 | async-start | bytes 2506752 | tf_op jit(solution)/shard_map/all_gather | solution.py:1487
  8.9 126.0 %all-gather.6.cloned.1.call-start = ((), (), s32[]{:S(2)}) async-start(), calls=%async_computation.3 | async-start | bytes 5013504 | tf_op jit(solution)/shard_map/all_gather | solution.py:1488
  9.0 29.0 %copy-start = (bf16[1,2048,768]{2,1,0:T(8,128)(2,1)S(1)}, bf16[1,2048,768]{2,1,0:T(8,128)(2,1)}, u32[]{:S(2)}) copy-start(bf16[1,2048,768]{2,1,0:T(8,128)(2,1)} %param.25) | copy-start | bytes 9437188
  37.9 332.5 %reduce-scatter.2.cloned.1.call-start = ((), (), s32[]{:S(2)}) async-start(), calls=%async_computation.2 | async-start | bytes 8773632 | tf_op jit(solution)/shard_map/reduce_scatter | solution.py:1512
  39.6 59.0 %collective-permute-start = (bf16[1536,768]{1,0:T(8,128)(2,1)}, bf16[1536,768]{1,0:T(8,128)(2,1)}, u32[]{:S(2)}, u32[]{:S(2)}) collective-permute-start(bf16[1536,768]{1,0:T(8,128)(2,1)} %slice_bitcast_fusion), channel_id=1, source_target_pairs={{16,0},{0,16},{17,1},{1,17},{18,2},{2,18},{19,3},{3,19},{20,4},{4,... | collective-permute-start | bytes 7077896 | tf_op jit(solution)/shard_map/ppermute | solution.py:1435
  269.4 82.2 %collective-permute-start.2 = (bf16[2,192,2048]{2,1,0:T(8,128)(2,1)}, bf16[2,192,2048]{2,1,0:T(8,128)(2,1)S(1)}, u32[]{:S(2)}, u32[]{:S(2)}) collective-permute-start(bf16[2,192,2048]{2,1,0:T(8,128)(2,1)} %get-tuple-element.160), channel_id=1, source_target_pairs={{16,0},{0,16},{17,1},{1,17},{18,2},{2,18},{19,3},{3,19},{20,4},{4,... | collective-permute-start | bytes 4718600 | tf_op jit(solution)/shard_map/ppermute | solution.py:1435
  299.0 52.6 %collective-permute-start.1 = (bf16[2,192,2048]{2,1,0:T(8,128)(2,1)}, bf16[2,192,2048]{2,1,0:T(8,128)(2,1)}, u32[]{:S(2)}, u32[]{:S(2)}) collective-permute-start(bf16[2,192,2048]{2,1,0:T(8,128)(2,1)} %get-tuple-element.159), channel_id=1, source_target_pairs={{16,0},{0,16},{17,1},{1,17},{18,2},{2,18},{19,3},{3,19},{20,4},{4,... | collective-permute-start | bytes 4718600 | tf_op jit(solution)/shard_map/ppermute | solution.py:1435
  351.6 18.8 %copy-start.1 = (bf16[2,192,2048]{2,1,0:T(8,128)(2,1)}, bf16[2,192,2048]{2,1,0:T(8,128)(2,1)S(1)}, u32[]{:S(2)}) copy-start(bf16[2,192,2048]{2,1,0:T(8,128)(2,1)S(1)} %collective-permute-done.2.refs_4_) | copy-start | bytes 4718596
Sparse Core Ops, SparseCore 0:
  10.9 45.5 all-gather.3
  58.8 52.2 all-gather.5
  241.8 128.5 reduce-scatter.1

commit v2 on v1

--- a/solution.py
+++ b/solution.py
@@ -621,7 +621,7 @@
             pltpu.VMEM(down, F32),
             pltpu.VMEM((rows, units), BF),
             pltpu.VMEM((rows, units), BF),
-            pltpu.VMEM((2, 5 * shard, width), BF),
+            pltpu.VMEM((6, 5 * shard, width), BF),
             pltpu.SemaphoreType.DMA((sharers,)),
             pltpu.VMEM(up, BF),
         ],
@@ -1421,7 +1421,7 @@
         ]
         + shares.scratch(),
         compiler_params=pltpu.CompilerParams(
-            collective_id=1, has_side_effects=True, vmem_limit_bytes=62 * MIB
+            collective_id=1, has_side_effects=True, vmem_limit_bytes=63 * MIB + MIB // 2
         ),
         cost_estimate=pl.CostEstimate(
             flops=4 * tokens * width * chains * ATT, bytes_accessed=30 * tokens * width, transcendentals=0

time: 423 us -> 431 us (1.019); the launches traced: 421 us -> 423 us
  no operation moved by 1% of the time
where the time goes in v2:
time: 431 us; the launch traced here: 423 us
  Pallas kernels  384 us (89%)
  waiting for transfers between devices  20.5 us (5%)
  between operations  14.9 us (3%)
    pallas_call x6, Pallas kernels, run_tiles(): pl.pallas_call(kernel, grid=(steps,), in_specs=list(in_specs), out_specs=...  142 us
    pallas_call x3, Pallas kernels, attend_back(): pl.pallas_call(functools.partial(attend_back_kernel, first, keys, queries...  108 us
    pallas_call x2, Pallas kernels, attend(): pl.pallas_call(functools.partial(attend_kernel, keys, queries, chunk, cou...  57 us
    pallas_call x1, Pallas kernels, finish(): pl.pallas_call(functools.partial(finish_kernel, blocks, rows, tiles, shar...  43.5 us
    pallas_call x1, Pallas kernels, gather_columns(): pl.pallas_call(functools.partial(gather_kernel, sharers, count, part, ear...  28.9 us
    reduce_scatter x1, waiting for transfers between devices, local(): mine = lax.psum_scatter(packed, 'dp', scatter_dimension=0, tiled=False)  20.4 us
  transfers between devices with their start and end apart: 6, of which 1 were waited for; matrix products, arithmetic and copies ran while one was open for 0% of the time, Pallas kernels for 55%

profile of v2, /device:TPU:0, one launch (start us, length us, event | category | flops | bytes accessed | tf_op | source)
XLA Modules:
  0.0 423.4 jit_solution(17895313554129996331)
XLA Ops:
  7.2 0.0 all-gather.4.cloned.1.call-start
  7.2 1.7 side_by_side.1
  8.9 0.0 all-gather.6.cloned.1.call-start
  9.0 28.9 %gather_columns.1 = (bf16[16,48,1408]{2,1,0:T(8,128)(2,1)}, f32[32,768]{1,0:T(8,128)}, f32[8,384]{1,0:T(8,128)}, f32[1,3072]{1,0:T(1,128)}, bf16[72,384]{1,0:T(8...) custom-call(f32[48,384]{1,0:T(8,128)} %refs_0_.2, ...), custom_call_target="tpu_custom_call" | custom-call | tf_op jit(solution)/shard_map/gather_columns/pallas_call | solution.py:980
  37.9 0.0 all-gather.6.cloned.1.call-update
  37.9 0.0 reduce-scatter.2.cloned.1.call-start
  38.0 1.6 slice_bitcast_fusion
  39.6 0.6 collective-permute-start
  40.8 8.6 %project.2 = (bf16[2048,384]{1,0:T(8,128)(2,1)}, bf16[384,2048]{1,0:T(8,128)(2,1)}, bf16[2048,384]{1,0:T(8,128)(2,1)}, bf16[384,2048]{1,0:T(8,128)(2,1)}, bf16[2...) custom-call(bf16[2048,768]{1,0:T(8,128)(2,1)} %bitcast.14, bf16[768,1408]{1,0:T(8,128)(2,1)} %bitcast.18, ...), custom_call_target="tpu_custom_call" | custom-call | flops 3623878656 | bytes 14774272 | tf_op jit(solution)/shard_map/project/pallas_call | solution.py:232
  49.4 28.5 %attend.2 = (f32[6,80,2048]{2,1,0:T(8,128)}, bf16[6,2048,2048]{2,1,0:T(8,128)(2,1)}) custom-call(s32[1]{0:T(128)S(6)} %copy.51.at_ref, bf16[384,2048]{1,0:T(8,128)(2,1)} %get-tuple-element.111.q_ref, bf16[2048,384]{1,0:T(8,128)(2,1)} %get-tuple-element.112.k_ref, bf16[384,2048]{1,0:T(8,128)(2,1)} %get-tuple-element.113.v_ref, ...), custom_call_target="tpu_custom_call" | custom-call | flops 786432 | bytes 24576 | tf_op jit(solution)/shard_map/attend/pallas_call | solution.py:115
  77.9 20.7 %mix.1 = (bf16[2048,768]{1,0:T(8,128)(2,1)}, f32[2048,384]{1,0:T(8,128)}, bf16[2048,384]{1,0:T(8,128)(2,1)}, f32[72,2048]{1,0:T(8,128)}, bf16[2048,128]{1,0:T(8,...) custom-call(bf16[2048,768]{1,0:T(8,128)(2,1)} %bitcast.15, ...), custom_call_target="tpu_custom_call" | custom-call | flops 9663676416 | bytes 21837824 | tf_op jit(solution)/shard_map/mix/pallas_call | solution.py:232
  98.5 7.7 %project.3 = (bf16[2048,384]{1,0:T(8,128)(2,1)}, bf16[384,2048]{1,0:T(8,128)(2,1)}, bf16[2048,384]{1,0:T(8,128)(2,1)}, bf16[384,2048]{1,0:T(8,128)(2,1)}, f32[8,512]{1,0:T(8,128)}) custom-call(bf16[512,768]{1,0:T(8,128)(2,1)} %get-tuple-element.116.refs_0_, bf16[1536,768]{1,0:T(8,128)(2,1)} %collective-permute-done.refs_1_, bf16[768,1408]{1,0:T(8,128)(2,1)} %bitcast.19, ...), custom_call_target="tpu_custom_call" | custom-call | flops 2415919104 | bytes 11628544 | tf_op jit(solution)/shard_map/project/pallas_call | solution.py:232
  106.2 28.6 %attend.3 = (f32[6,80,2048]{2,1,0:T(8,128)}, bf16[6,2048,2048]{2,1,0:T(8,128)(2,1)}) custom-call(s32[1]{0:T(128)S(6)} %copy.51.at_ref, bf16[384,2048]{1,0:T(8,128)(2,1)} %get-tuple-element.111.q_ref, bf16[2048,384]{1,0:T(8,128)(2,1)} %get-tuple-element.124.k_ref, bf16[384,2048]{1,0:T(8,128)(2,1)} %get-tuple-element.125.v_ref, ...), custom_call_target="tpu_custom_call" | custom-call | flops 786432 | bytes 24576 | tf_op jit(solution)/shard_map/attend/pallas_call | solution.py:115
  134.8 70.8 %middle.1 = (bf16[2048,768]{1,0:T(8,128)(2,1)}, f32[2048,768]{1,0:T(8,128)}, bf16[2048,384]{1,0:T(8,128)(2,1)}, bf16[384,2048]{1,0:T(8,128)(2,1)}, bf16[384,2048...) custom-call(f32[6,80,2048]{2,1,0:T(8,128)} %get-tuple-element.115.re, ...), custom_call_target="tpu_custom_call" | custom-call | flops 36238786560 | bytes 46239744 | tf_op jit(solution)/shard_map/middle/pallas_call | solution.py:232
  205.7 32.3 %mix_back.1 = (bf16[2048,384]{1,0:T(8,128)(2,1)}, bf16[2048,768]{1,0:T(8,128)(2,1)}, bf16[2080,384]{1,0:T(8,128)(2,1)}, bf16[16,336,768]{2,1,0:T(8,128)(2,1)}, bf16[768,2048]{1,0:T(8,128)(2,1)}) custom-call(bf16[2048,768]{1,0:T(8,128)(2,1)} %bitcast.17, bf16[32,768]{1,0:T(8,128)(2,1)} %get-tuple-element.117.halo_ref, ...), custom_call_target="tpu_custom_call", output_to_operand_aliasing={{3}: (15, {})} | custom-call | flops 9663676416 | bytes 45430784 | tf_op jit(solution)/shard_map/mix_back/pallas_call | solution.py:232
  238.0 0.0 reduce-scatter.2.cloned.1.call-update
  238.0 27.8 %attend_back.4 = (bf16[192,2048]{1,0:T(8,128)(2,1)}, bf16[2,192,2048]{2,1,0:T(8,128)(2,1)}) custom-call(bf16[6,2048,2048]{2,1,0:T(8,128)(2,1)} %get-tuple-element.132.p_ref, bf16[2048,384]{1,0:T(8,128)(2,1)} %get-tuple-element.133.v_ref, bf16[384,2048]{1,0:T(8,128)(2,1)} %get-tuple-element.134.kt_ref, bf16[384,2048]{1,0:T(8,128)(2,1)} %get-tuple-element.135.g_ref, ...), custom_call_target="tpu_custom_call" | custom-call | flops 25769803776 | bytes 25165824 | tf_op jit(solution)/shard_map/attend_back/pallas_call | solution.py:181
  265.8 1.4 collective-permute-start.2
  267.2 27.9 %attend_back.3 = (bf16[192,2048]{1,0:T(8,128)(2,1)}, bf16[2,192,2048]{2,1,0:T(8,128)(2,1)}) custom-call(bf16[6,2048,2048]{2,1,0:T(8,128)(2,1)} %get-tuple-element.132.p_ref, bf16[2048,384]{1,0:T(8,128)(2,1)} %get-tuple-element.133.v_ref, bf16[384,2048]{1,0:T(8,128)(2,1)} %get-tuple-element.134.kt_ref, bf16[384,2048]{1,0:T(8,128)(2,1)} %get-tuple-element.135.g_ref, ...), custom_call_target="tpu_custom_call" | custom-call | flops 25769803776 | bytes 25165824 | tf_op jit(solution)/shard_map/attend_back/pallas_call | solution.py:181
  295.1 0.6 collective-permute-start.1
  295.7 52.6 %attend_back.5 = (bf16[384,2048]{1,0:T(8,128)(2,1)}, bf16[2,384,2048]{2,1,0:T(8,128)(2,1)}) custom-call(bf16[6,2048,2048]{2,1,0:T(8,128)(2,1)} %get-tuple-element.153.p_ref, bf16[2048,384]{1,0:T(8,128)(2,1)} %get-tuple-element.154.v_ref, bf16[384,2048]{1,0:T(8,128)(2,1)} %get-tuple-element.155.kt_ref, bf16[384,2048]{1,0:T(8,128)(2,1)} %get-tuple-element.156.g_ref, ...), custom_call_target="tpu_custom_call" | custom-call | flops 51539607552 | bytes 50331648 | tf_op jit(solution)/shard_map/attend_back/pallas_call | solution.py:181
  348.3 20.4 %reduce-scatter.2.cloned.1.call-done = bf16[1,336,768]{2,1,0:T(8,128)(2,1)} async-done(((bf16[16,336,768]{2,1,0:T(8,128)(2,1)}), bf16[1,336,768]{2,1,0:T(8,128)(2,1)}) %reduce-scatter.2.cloned.1.call-update) | async-done | bytes 516112 | tf_op jit(solution)/shard_map/reduce_scatter | solution.py:1512
  368.7 43.5 %finish.1 = (bf16[2048,768]{1,0:T(8,128)(2,1)}, f32[336,768]{1,0:T(8,128)}, f32[48,1280]{1,0:T(8,128)}) custom-call(bf16[192,2048]{1,0:T(8,128)(2,1)} %get-tuple-element.151.refs_0_, bf16[192,2048]{1,0:T(8,128)(2,1)} %get-tuple-element.152.refs_1_, bf16[384,2048]{1,0:T(8,128)(2,1)} %get-tuple-element.158.refs_2_, ...), custom_call_target="tpu_custom_call" | custom-call | flops 7247757312 | bytes 47185920 | tf_op jit(solution)/shard_map/finish/pallas_call | solution.py:1400
  412.2 4.2 unpack.1
  (8 shorter events, 0.0 us)
Async XLA Ops:
  7.2 70.7 %all-gather.4.cloned.1.call-start = ((), (), s32[]{:S(2)}) async-start(), calls=%async_computation.1 | async-start | bytes 2506752 | tf_op jit(solution)/shard_map/all_gather | solution.py:1487
  8.9 125.9 %all-gather.6.cloned.1.call-start = ((), (), s32[]{:S(2)}) async-start(), calls=%async_computation.3 | async-start | bytes 5013504 | tf_op jit(solution)/shard_map/all_gather | solution.py:1488
  9.0 29.0 %copy-start = (bf16[1,2048,768]{2,1,0:T(8,128)(2,1)S(1)}, bf16[1,2048,768]{2,1,0:T(8,128)(2,1)}, u32[]{:S(2)}) copy-start(bf16[1,2048,768]{2,1,0:T(8,128)(2,1)} %param.25) | copy-start | bytes 9437188
  37.9 330.8 %reduce-scatter.2.cloned.1.call-start = ((), (), s32[]{:S(2)}) async-start(), calls=%async_computation.2 | async-start | bytes 8773632 | tf_op jit(solution)/shard_map/reduce_scatter | solution.py:1512
  39.6 59.0 %collective-permute-start = (bf16[1536,768]{1,0:T(8,128)(2,1)}, bf16[1536,768]{1,0:T(8,128)(2,1)}, u32[]{:S(2)}, u32[]{:S(2)}) collective-permute-start(bf16[1536,768]{1,0:T(8,128)(2,1)} %slice_bitcast_fusion), channel_id=1, source_target_pairs={{16,0},{0,16},{17,1},{1,17},{18,2},{2,18},{19,3},{3,19},{20,4},{4,... | collective-permute-start | bytes 7077896 | tf_op jit(solution)/shard_map/ppermute | solution.py:1435
  265.8 82.5 %collective-permute-start.2 = (bf16[2,192,2048]{2,1,0:T(8,128)(2,1)}, bf16[2,192,2048]{2,1,0:T(8,128)(2,1)}, u32[]{:S(2)}, u32[]{:S(2)}) collective-permute-start(bf16[2,192,2048]{2,1,0:T(8,128)(2,1)} %get-tuple-element.160), channel_id=1, source_target_pairs={{16,0},{0,16},{17,1},{1,17},{18,2},{2,18},{19,3},{3,19},{20,4},{4,... | collective-permute-start | bytes 4718600 | tf_op jit(solution)/shard_map/ppermute | solution.py:1435
  295.1 53.2 %collective-permute-start.1 = (bf16[2,192,2048]{2,1,0:T(8,128)(2,1)}, bf16[2,192,2048]{2,1,0:T(8,128)(2,1)}, u32[]{:S(2)}, u32[]{:S(2)}) collective-permute-start(bf16[2,192,2048]{2,1,0:T(8,128)(2,1)} %get-tuple-element.159), channel_id=1, source_target_pairs={{16,0},{0,16},{17,1},{1,17},{18,2},{2,18},{19,3},{3,19},{20,4},{4,... | collective-permute-start | bytes 4718600 | tf_op jit(solution)/shard_map/ppermute | solution.py:1435
Sparse Core Ops, SparseCore 0:
  10.9 45.5 all-gather.3
  58.8 52.2 all-gather.5
  238.1 130.5 reduce-scatter.1
